TPU v7x, 256 devices: a whole 4x4x8 slice. The times are simulated.
256 devices in a mesh: occ: 16 (over x, y), vr: 8 (over z), vc: 2 (over core).
Axes of the slice: x: 4, y: 4, z: 8, core: 2. Of those that a mesh axis runs over, the one named last changes fastest.
Arguments:
- ladder_amps: float32 [1024, 12288], P('occ', ('vr', 'vc')), may hold values from -6 to 6
- vvvv_slice: float32 [12288, 47104], P('occ', ('vr', 'vc')), may hold values from -0.0546875 to 0.0546875
- cd_live: int32 [192], P('occ'), may hold values 0 or 1
- amplitudes: float32 [1024, 47104], P('occ', ('vr', 'vc')), may hold values from -6 to 6
- hole_inter: float32 [1024, 1024], P('occ', ('vr', 'vc')), may hold values from -0.1875 to 0.1875
- direct: float32 [1024, 47104], P('occ', ('vr', 'vc')), may hold values from -6 to 6
- occ_energy: float32 [1024], P('occ'), may hold values from -3 to -1
- vir_energy: float32 [47104], P(('vr', 'vc')), may hold values from 1 to 4
Outputs:
- new_amps: float32 [1024, 47104], P('occ', ('vr', 'vc'))
All inputs are finite; a program needn't handle non-finite values. No bound on the sum of `cd_live` on one device may be relied on, other than what follows from the above.
Results may differ from a plain program's by a relative error of at most 0.000057.
Values sent between devices are 32-bit elements; how exact they have to be, the bound alone decides.
No kernel may reach another device: no remote copies, remote signals or barrier semaphores. Data moves between devices by JAX's collectives and lax.ppermute only.
A program may use at most 128 MiB of HBM per device.

v0:
```python
import jax
import jax.numpy as jnp
from jax import lax
from jax.sharding import PartitionSpec as P

BLOCK = 64


def on_device(
    ladder_amps, vvvv_slice, cd_live, amplitudes, hole_inter, direct, occ_energy, vir_energy
):
    highest = lax.Precision.HIGHEST
    amp_slab, inter_rows = (
        lax.all_gather(ladder_amps, ("vr", "vc"), axis=1, tiled=True),
        lax.all_gather(hole_inter, ("vr", "vc"), axis=1, tiled=True),
    )
    live_cols = jnp.repeat(cd_live.astype(jnp.float32), BLOCK)
    columns = lax.all_to_all(amp_slab, "occ", split_axis=1, concat_axis=0, tiled=True)
    masked = columns * live_cols[None, :]
    ladder_terms = jnp.dot(
        masked, vvvv_slice, precision=highest, preferred_element_type=jnp.float32
    )
    ladder = lax.psum_scatter(ladder_terms, "occ", scatter_dimension=0, tiled=True)
    hole_term = jnp.dot(
        inter_rows,
        lax.all_gather(amplitudes, "occ", axis=0, tiled=True),
        precision=highest,
        preferred_element_type=jnp.float32,
    )
    summed = ladder + hole_term
    residue = direct + summed
    return residue / (vir_energy[None, :] - occ_energy[:, None])


def solution(mesh):
    in_specs = (
        P("occ", ("vr", "vc")),
        P("occ", ("vr", "vc")),
        P("occ"),
        P("occ", ("vr", "vc")),
        P("occ", ("vr", "vc")),
        P("occ", ("vr", "vc")),
        P("occ"),
        P(("vr", "vc")),
    )
    out_specs = P("occ", ("vr", "vc"))
    return jax.shard_map(
        on_device, mesh=mesh, in_specs=in_specs, out_specs=out_specs, check_vma=False
    )
```

profile of v0, /device:TPU:8, one launch (start us, length us, event | category | flops | bytes accessed | tf_op | source)
XLA Modules:
  0.0 296.3 jit_solution(10751177651908895084)
XLA Ops:
  6.5 0.0 copy-start.4
  6.5 0.0 all-gather.3.cloned.1.call-start
  6.5 0.7 all-gather.3.cloned.1.call-update
  7.3 0.0 all-gather.5.cloned.1.call-start
  7.3 0.7 all-gather.5.cloned.1.call-update
  8.0 45.1 %all-gather.3.cloned.1.call-done = f32[64,12288]{1,0:T(8,128)} async-done(((f32[64,768]{1,0:T(8,128)}), f32[64,12288]{1,0:T(8,128)}) %all-gather.3.cloned.1.call-update) | async-done | bytes 3145744 | tf_op jit(solution)/shard_map/all_gather | solution.py:14
  53.1 3.9 %copy.14 = f32[8,16,8,768]{3,2,0,1:T(8,128)} copy(f32[8,16,8,768]{3,2,1,0:T(8,128)} %bitcast.12) | data formatting | bytes 6291456 | tf_op jit(solution)/shard_map/all_to_all | solution.py:18
  57.0 7.3 %all-to-all-start = ((f32[64,16,768]{2,0,1:T(8,128)}), f32[64,16,768]{2,0,1:T(8,128)S(1)}, u32[]{:S(2)}, u32[]{:S(2)}) async-start(f32[64,16,768]{2,0,1:T(8,128)} %bitcast.11), calls=%async_computation | async-start | bytes 6291456 | tf_op jit(solution)/shard_map/all_to_all | solution.py:18
  64.2 0.0 reduce-scatter.2.cloned.1.call-start
  64.3 0.0 copy-done.4
  64.3 0.1 broadcast_in_dim.2
  64.4 0.1 mul.10
  64.5 52.1 %all-to-all-done = f32[64,16,768]{2,0,1:T(8,128)S(1)} async-done(((f32[64,16,768]{2,0,1:T(8,128)}), f32[64,16,768]{2,0,1:T(8,128)S(1)}, u32[]{:S(2)}, u32[]{:S(2)}) %all-to-all-start) | async-done | bytes 3145760 | tf_op jit(solution)/shard_map/all_to_all | solution.py:18
  116.6 0.2 bitcast_multiply_fusion
  116.8 34.3 %fusion.2 = f32[1024,2944]{1,0:T(8,128)} fusion(f32[1024,768]{1,0:T(8,128)S(1)} %bitcast_multiply_fusion, f32[768,2944]{1,0:T(8,128)} %param.9), kind=kOutput, calls=%fused_computation.5 | convolution fusion | flops 27783069696 | bytes 24248320 | tf_op jit(solution)/shard_map/dot_general | solution.py:20
  151.1 0.0 copy-start.1
  151.1 0.0 copy-start
  151.1 0.0 copy-start.2
  151.1 0.0 copy-start.3
  151.1 0.0 reduce-scatter.2.cloned.1.call-update
  151.2 0.7 copy-done.1
  151.9 0.1 copy.11
  152.0 17.2 %all_gather.10 = f32[64,1024]{0,1:T(8,128)S(1)} all-gather(f32[64,64]{0,1:T(8,128)S(1)} %copy.11), channel_id=1, replica_groups=mesh['occ'=16,'vr'=8,'vc'=2] {'vr','vc'}, dimensions={1}, use_global_device_ids=true | all-gather | bytes 278528 | tf_op jit(solution)/shard_map/all_gather | solution.py:15
  169.2 9.1 %all-gather.5.cloned.1.call-done = f32[1024,2944]{1,0:T(8,128)} async-done(((f32[64,2944]{1,0:T(8,128)}), f32[1024,2944]{1,0:T(8,128)}) %all-gather.5.cloned.1.call-update) | async-done | bytes 12058640 | tf_op jit(solution)/shard_map/all_gather | solution.py:26
  178.2 100.9 %reduce-scatter.2.cloned.1.call-done = f32[64,2944]{1,0:T(8,128)} async-done(((f32[1024,2944]{1,0:T(8,128)}), f32[64,2944]{1,0:T(8,128)}) %reduce-scatter.2.cloned.1.call-update) | async-done | bytes 753680 | tf_op jit(solution)/shard_map/reduce_scatter | solution.py:23
  279.2 0.0 copy-done
  279.2 0.0 copy-done.2
  279.2 0.0 copy-done.3
  279.2 10.6 %fusion.1 = f32[64,2944]{1,0:T(8,128)} fusion(f32[64,2944]{1,0:T(8,128)S(1)} %copy-done, f32[64,2944]{1,0:T(8,128)} %reduce-scatter.2.cloned.1.call-done, f32[64,1024]{0,1:T(8,128)S(1)} %all_gather.10, f32[1024,2944]{1,0:T(8,128)} %all-gather.5.cloned.1.call-done, f32[64]{0:T(128)S(1)} %copy-done.3, f32[2944]{0:T(1024)S(1)} %copy-done.2), kind=kOutput, calls=%fused_computation.2 | convolution fusion | flops 2316009472 | bytes 14593792 | tf_op jit(solution)/shard_map/dot_general | solution.py:24
  (1 shorter events, 0.0 us)
Async XLA Ops:
  6.5 57.8 %copy-start.4 = (s32[12]{0:T(128)S(1)}, s32[12]{0:T(128)}, u32[]{:S(2)}) copy-start(s32[12]{0:T(128)} %param.10) | copy-start | bytes 148
  6.5 46.6 %all-gather.3.cloned.1.call-start = ((), (), s32[]{:S(2)}) async-start(), calls=%async_computation.2 | async-start | bytes 3342336 | tf_op jit(solution)/shard_map/all_gather | solution.py:14
  7.3 171.0 %all-gather.5.cloned.1.call-start = ((), (), s32[]{:S(2)}) async-start(), calls=%async_computation.4 | async-start | bytes 12812288 | tf_op jit(solution)/shard_map/all_gather | solution.py:26
  57.0 59.6 %all-to-all-start = ((f32[64,16,768]{2,0,1:T(8,128)}), f32[64,16,768]{2,0,1:T(8,128)S(1)}, u32[]{:S(2)}, u32[]{:S(2)}) async-start(f32[64,16,768]{2,0,1:T(8,128)} %bitcast.11), calls=%async_computation | async-start | bytes 6291456 | tf_op jit(solution)/shard_map/all_to_all | solution.py:18
  64.2 214.9 %reduce-scatter.2.cloned.1.call-start = ((), (), s32[]{:S(2)}) async-start(), calls=%async_computation.3 | async-start | bytes 12812288 | tf_op jit(solution)/shard_map/reduce_scatter | solution.py:23
  151.1 0.8 copy-start.1
  151.1 128.1 %copy-start = (f32[64,2944]{1,0:T(8,128)S(1)}, f32[64,2944]{1,0:T(8,128)}, u32[]{:S(2)}) copy-start(f32[64,2944]{1,0:T(8,128)} %param.13) | copy-start | bytes 2260996
  151.1 128.1 %copy-start.2 = (f32[2944]{0:T(1024)S(1)}, f32[2944]{0:T(1024)}, u32[]{:S(2)}) copy-start(f32[2944]{0:T(1024)} %param.15) | copy-start | bytes 35332
  151.1 128.1 %copy-start.3 = (f32[64]{0:T(128)S(1)}, f32[64]{0:T(128)}, u32[]{:S(2)}) copy-start(f32[64]{0:T(128)} %param.14) | copy-start | bytes 772
Sparse Core Ops, SparseCore 0:
  9.2 43.8 all-gather.2
  55.6 122.6 all-gather.4
  182.0 97.0 reduce-scatter.1
where the time goes:
time: 298 us; the launch traced here: 296 us
  waiting for transfers between devices  209 us (70%)
  matrix products  44.9 us (15%)
  blocking collectives  17.2 us (6%)
  between operations  13.1 us (4%)
  starting transfers between devices  7.33 us (2%)
  local copies, waits for them, and re-layouts  4.83 us (2%)
    reduce_scatter x1, waiting for transfers between devices, on_device(): lax.psum_scatter(ladder_terms, 'occ', scatter_dimension=0, tiled=True)  101 us
    all_to_all x1, waiting for transfers between devices, on_device(): lax.all_to_all(amp_slab, 'occ', split_axis=1, concat_axis=0, tiled=True)  52.1 us
    all_gather x1, waiting for transfers between devices, on_device(): lax.all_gather(ladder_amps, ('vr', 'vc'), axis=1, tiled=True)  45.1 us
    dot_general x1, matrix products, on_device(): jnp.dot(masked, vvvv_slice, precision=highest, preferred_element_type=jnp...  34.3 us
    all_gather x1, blocking collectives, on_device(): lax.all_gather(hole_inter, ('vr', 'vc'), axis=1, tiled=True)  17.2 us
    dot_general x1, matrix products, on_device(): jnp.dot(inter_rows, lax.all_gather(amplitudes, 'occ', axis=0, tiled=True)...  10.6 us
    all_gather x1, waiting for transfers between devices, on_device(): lax.all_gather(amplitudes, 'occ', axis=0, tiled=True)  9.06 us
    all_to_all x1, starting transfers between devices, on_device(): lax.all_to_all(amp_slab, 'occ', split_axis=1, concat_axis=0, tiled=True)  7.26 us
  transfers between devices with their start and end apart: 4, of which 4 were waited for; matrix products, arithmetic and copies ran while one was open for 13% of the time, Pallas kernels for 0%

commit v1 on v0

v1 whole, which is shorter than its diff:
```python
import jax
import jax.numpy as jnp
from jax import lax
from jax.sharding import PartitionSpec as P

BLOCK = 64


def on_device(
    ladder_amps, vvvv_slice, cd_live, amplitudes, hole_inter, direct, occ_energy, vir_energy
):
    n = lax.axis_size("occ")
    swap = [(o * n + c, c * n + o) for o in range(n) for c in range(n)]
    mine = jnp.concatenate([ladder_amps, hole_inter], axis=1)
    mine = lax.ppermute(mine, ("occ", "vr", "vc"), swap)
    live_cols = jnp.repeat(cd_live.astype(jnp.float32), BLOCK)
    keep = jnp.concatenate([live_cols, jnp.ones((hole_inter.shape[1],), jnp.float32)])
    left = lax.all_gather(mine * keep[None, :], ("vr", "vc"), axis=0, tiled=True)
    right = jnp.concatenate([vvvv_slice, amplitudes], axis=0)
    terms = jnp.dot(left, right, precision=lax.Precision.HIGH, preferred_element_type=jnp.float32)
    summed = lax.psum_scatter(terms, "occ", scatter_dimension=0, tiled=True)
    return (direct + summed) / (vir_energy[None, :] - occ_energy[:, None])


def solution(mesh):
    in_specs = (
        P("occ", ("vr", "vc")),
        P("occ", ("vr", "vc")),
        P("occ"),
        P("occ", ("vr", "vc")),
        P("occ", ("vr", "vc")),
        P("occ", ("vr", "vc")),
        P("occ"),
        P(("vr", "vc")),
    )
    out_specs = P("occ", ("vr", "vc"))
    return jax.shard_map(
        on_device, mesh=mesh, in_specs=in_specs, out_specs=out_specs, check_vma=False
    )
```

time: 298 us -> 211 us (0.71)
  waiting for transfers between devices: 209 us -> 164 us
  matrix products: 44.9 us -> 25 us
  blocking collectives: 17.2 us -> 0 us
  starting transfers between devices: 7.33 us -> 1.96 us
  local copies, waits for them, and re-layouts: 4.83 us -> 0.16 us
  other arithmetic: 0.21 us -> 4.49 us
    all_to_all x1 -> x0, waiting for transfers between devices: 52.1 us -> none  [on_device(): lax.all_to_all(amp_slab, 'occ', split_axis=1, concat_axis=0, tiled=True)]
    dot_general x2 -> x1, matrix products: 44.9 us -> 25 us  [on_device(): jnp.dot(left, right, precision=lax.Precision.HIGH, preferred_element_type...]
    all_gather x1 -> x0, blocking collectives: 17.2 us -> none  [on_device(): lax.all_gather(hole_inter, ('vr', 'vc'), axis=1, tiled=True)]
    all_gather x2 -> x1, waiting for transfers between devices: 54.2 us -> 63.6 us  [on_device(): lax.all_gather(mine * keep[None, :], ('vr', 'vc'), axis=0, tiled=True)]
    all_to_all x1 -> x0, starting transfers between devices: 7.26 us -> none  [on_device(): lax.all_to_all(amp_slab, 'occ', split_axis=1, concat_axis=0, tiled=True)]
    reduce_scatter x1, waiting for transfers between devices: 101 us -> 96.3 us  [on_device(): summed = lax.psum_scatter(terms, 'occ', scatter_dimension=0, tiled=True)]
    ppermute x0 -> x1, waiting for transfers between devices: none -> 4.6 us  [on_device(): mine = lax.ppermute(mine, ('occ', 'vr', 'vc'), swap)]
    all_to_all x1 -> x0, local copies, waits for them, and re-layouts: 3.88 us -> none  [on_device(): lax.all_to_all(amp_slab, 'occ', split_axis=1, concat_axis=0, tiled=True)]
  transfers between devices with their start and end apart: 4 -> 3, of which waited for: 4 -> 3; matrix products, arithmetic and copies ran while one was open for 13% -> 0% of each run, Pallas kernels for 0% -> 0%
where the time goes in v1:
time: 211 us; the launch traced here: 210 us
  waiting for transfers between devices  164 us (78%)
  matrix products  25 us (12%)
  between operations  13.4 us (6%)
  other arithmetic  4.49 us (2%)
    reduce_scatter x1, waiting for transfers between devices, on_device(): summed = lax.psum_scatter(terms, 'occ', scatter_dimension=0, tiled=True)  96.3 us
    all_gather x1, waiting for transfers between devices, on_device(): lax.all_gather(mine * keep[None, :], ('vr', 'vc'), axis=0, tiled=True)  63.6 us
    dot_general x1, matrix products, on_device(): jnp.dot(left, right, precision=lax.Precision.HIGH, preferred_element_type...  25 us
    ppermute x1, waiting for transfers between devices, on_device(): mine = lax.ppermute(mine, ('occ', 'vr', 'vc'), swap)  4.6 us
  transfers between devices with their start and end apart: 3, of which 3 were waited for; matrix products, arithmetic and copies ran while one was open for 0% of the time, Pallas kernels for 0%

profile of v1, /device:TPU:8, one launch (start us, length us, event | category | flops | bytes accessed | tf_op | source)
XLA Modules:
  0.0 209.6 jit_solution(2977284989686135115)
XLA Ops:
  6.5 0.0 all-gather.2.cloned.1.call-start
  6.5 1.0 pad_maximum_fusion
  7.5 1.9 collective-permute-start
  9.4 0.7 convert_element_type.3
  10.1 0.1 broadcast_in_dim.2
  10.2 0.1 reshape.6
  10.2 4.6 %collective-permute-done = f32[64,832]{1,0:T(8,128)S(1)} collective-permute-done((f32[64,832]{1,0:T(8,128)S(1)}, f32[64,832]{1,0:T(8,128)S(1)}, u32[]{:S(2)}, u32[]{:S(2)}) %collective-permute-start) | collective-permute-done | bytes 213024 | tf_op jit(solution)/shard_map/ppermute | solution.py:15
  14.8 0.7 broadcast_multiply_fusion
  15.6 0.0 all-gather.2.cloned.1.call-update
  15.6 0.0 reduce-scatter.2.cloned.1.call-start
  15.6 63.6 %all-gather.2.cloned.1.call-done = f32[1024,832]{1,0:T(8,128)} async-done(((f32[64,832]{1,0:T(8,128)}), f32[1024,832]{1,0:T(8,128)}) %all-gather.2.cloned.1.call-update) | async-done | bytes 3407888 | tf_op jit(solution)/shard_map/all_gather | solution.py:18
  79.2 25.0 %fusion = f32[1024,2944]{1,0:T(8,128)} fusion(f32[1024,832]{1,0:T(8,128)} %all-gather.2.cloned.1.call-done, f32[64,2944]{1,0:T(8,128)} %param.11, f32[768,2944]{1,0:T(8,128)} %param.9), kind=kOutput, calls=%fused_computation | convolution fusion | flops 15051612160 | bytes 25264128 | tf_op jit(solution)/shard_map/dot_general | solution.py:20
  104.2 0.0 copy-start
  104.2 0.0 copy-start.1
  104.2 0.0 copy-start.2
  104.2 0.0 reduce-scatter.2.cloned.1.call-update
  104.3 96.3 %reduce-scatter.2.cloned.1.call-done = f32[64,2944]{1,0:T(8,128)} async-done(((f32[1024,2944]{1,0:T(8,128)}), f32[64,2944]{1,0:T(8,128)}) %reduce-scatter.2.cloned.1.call-update) | async-done | bytes 753680 | tf_op jit(solution)/shard_map/reduce_scatter | solution.py:21
  200.5 0.0 copy-done
  200.5 0.0 copy-done.1
  200.6 0.0 copy-done.2
  200.6 2.2 %subtract_divide_fusion = f32[64,2944]{1,0:T(8,128)} fusion(f32[64,2944]{1,0:T(8,128)S(1)} %copy-done, f32[64,2944]{1,0:T(8,128)} %reduce-scatter.2.cloned.1.call-done, f32[64]{0:T(128)S(1)} %copy-done.2, f32[2944]{0:T(1024)S(1)} %copy-done.1), kind=kLoop, calls=%fused_computation.4 | loop fusion | flops 565248 | bytes 2273024 | tf_op jit(solution)/shard_map/div | solution.py:22
  (1 shorter events, 0.0 us)
Async XLA Ops:
  6.5 72.7 %all-gather.2.cloned.1.call-start = ((), (), s32[]{:S(2)}) async-start(), calls=%async_computation.1 | async-start | bytes 3899392 | tf_op jit(solution)/shard_map/all_gather | solution.py:18
  7.5 7.3 %collective-permute-start = (f32[64,832]{1,0:T(8,128)S(1)}, f32[64,832]{1,0:T(8,128)S(1)}, u32[]{:S(2)}, u32[]{:S(2)}) collective-permute-start(f32[64,832]{1,0:T(8,128)S(1)} %pad_maximum_fusion), channel_id=1, source_target_pairs={{0,0},{1,16},{2,32},{3,48},{4,64},{5,80},{6,96},{7,112},{8,128},{9... | collective-permute-start | bytes 638984 | tf_op jit(solution)/shard_map/ppermute | solution.py:15
  15.6 185.0 %reduce-scatter.2.cloned.1.call-start = ((), (), s32[]{:S(2)}) async-start(), calls=%async_computation.2 | async-start | bytes 12812288 | tf_op jit(solution)/shard_map/reduce_scatter | solution.py:21
  104.2 96.3 %copy-start = (f32[64,2944]{1,0:T(8,128)S(1)}, f32[64,2944]{1,0:T(8,128)}, u32[]{:S(2)}) copy-start(f32[64,2944]{1,0:T(8,128)} %param.13) | copy-start | bytes 2260996
  104.2 96.3 %copy-start.1 = (f32[2944]{0:T(1024)S(1)}, f32[2944]{0:T(1024)}, u32[]{:S(2)}) copy-start(f32[2944]{0:T(1024)} %param.15) | copy-start | bytes 35332
  104.2 96.3 %copy-start.2 = (f32[64]{0:T(128)S(1)}, f32[64]{0:T(128)}, u32[]{:S(2)}) copy-start(f32[64]{0:T(128)} %param.14) | copy-start | bytes 772
Sparse Core Ops, SparseCore 0:
  15.7 63.4 all-gather.1
  104.4 96.1 reduce-scatter.1

commit v2 on v1

v2 whole, which is shorter than its diff:
```python
import functools

import jax
import jax.numpy as jnp
import numpy as np
from jax import lax
from jax.experimental import pallas as pl
from jax.experimental.pallas import tpu as pltpu
from jax.sharding import PartitionSpec as P

BLOCK = 64
AXES = ("occ", "vr", "vc")
NX, NY, NZ, NC = 4, 4, 8, 2
TILE = 512
COST = 1000
SIZES = (64,)
ROUNDS = ((0, 3), (3, 6))
ORDER = (
    (2, 0), (2, 1), (1, 2), (1, 3),
    (2, 2), (2, 3), (3, 0), (3, 1),
    (1, 0), (1, 1),
    (3, 2), (3, 3),
    (0, 0), (0, 1), (0, 2), (0, 3),
)
PARTS = (4, 4, 2, 2, 4)


def place(x, y, z, k):
    return (((x % NX) * NY + y % NY) * NZ + z % NZ) * NC + k % NC


def pairs(fn):
    out = []
    for x in range(NX):
        for y in range(NY):
            for z in range(NZ):
                for k in range(NC):
                    out.append((place(x, y, z, k), place(*fn(x, y, z, k))))
    return out


def first(d):
    return pairs(lambda x, y, z, k: (x + d, y, z, k) if k == 0 else (x, y + d, z, k))


def second(d):
    return pairs(lambda x, y, z, k: (x, y + d, z, k) if k == 0 else (x + d, y, z, k))


FROM = (6, 3, 4, 7, 4, 1, 0, 6, 0, 4, 6, 2, 3, 7, 1, 5)
TO = (3, 1, 0, 2, 2, 4, 7, 6, 1, 6, 0, 5, 7, 5, 3, 4)
CORE = (1, 1, 0, 1, 0, 1, 0, 0, 0, 1, 1, 1, 1, 0, 0, 0)


def to_slots(x, y, z, k):
    c, o = z * NC + k, x * NY + y
    return c // NY, c % NY, FROM[c] + TO[o], CORE[o]


def places():
    table = np.zeros((NX * NY * NZ * NC, len(ORDER)), np.int32)
    for x in range(NX):
        for y in range(NY):
            for z in range(NZ):
                for k in range(NC):
                    for q, (a, b) in enumerate(ORDER):
                        o = (x + a) % NX * NY + (y + b) % NY if k == 0 else (x + b) % NX * NY + (y + a) % NY
                        home = FROM[x * NY + y] + TO[o]
                        steps = (z - home if k == 0 else home - z) % NZ
                        other = int(CORE[o] != k)
                        if steps < 4:
                            at = 2 * steps + other
                        elif steps == 4:
                            at = 15 if other else 8
                        else:
                            at = 9 + 2 * (NZ - 1 - steps) + 1 - other
                        table[place(x, y, z, k), q] = at
    return table


SLOTS = pairs(to_slots)
ALONG_Z = pairs(lambda x, y, z, k: (x, y, z + (1 if k == 0 else -1), k))
OTHER = pairs(lambda x, y, z, k: (x, y, z, 1 - k))


def send(x, p):
    return lax.ppermute(x, AXES, p)


def split(x):
    hi = x.astype(jnp.bfloat16)
    return hi, (x - hi.astype(jnp.float32)).astype(jnp.bfloat16)


def prepare_kernel(v_ref, a_ref, hi_ref, lo_ref, tail_ref):
    hi, lo = split(v_ref[...])
    hi_ref[...] = hi
    lo_ref[...] = lo
    ah, al = split(a_ref[...])
    tail_ref[...] = jnp.concatenate([ah, al, ah], axis=0)


def prepare(v, a):
    v = pltpu.with_memory_space_constraint(v, pltpu.HBM)
    cd, n = v.shape
    o = a.shape[0]
    col = lambda i: (0, i)
    return pl.pallas_call(
        prepare_kernel,
        grid=(pl.cdiv(n, TILE),),
        in_specs=[pl.BlockSpec((cd, TILE), col), pl.BlockSpec((o, TILE), col)],
        out_specs=[pl.BlockSpec((cd, TILE), col), pl.BlockSpec((cd, TILE), col), pl.BlockSpec((3 * o, TILE), col)],
        out_shape=[
            pltpu.HBM((cd, n), jnp.bfloat16),
            pltpu.HBM((cd, n), jnp.bfloat16),
            pltpu.HBM((3 * o, n), jnp.bfloat16),
        ],
        compiler_params=pltpu.CompilerParams(vmem_limit_bytes=32 << 20),
        cost_estimate=pl.CostEstimate(flops=4 * cd * n, bytes_accessed=8 * (cd + o) * n, transcendentals=0),
        name="prepare",
    )(v, a)


def product_kernel(n_src, cd, parts, idx_ref, *refs):
    x_refs, (keep_ref, hi_ref, lo_ref, tail_ref) = refs[:n_src], refs[n_src : n_src + 4]
    outs, (x_all, lh, ll, lt) = refs[n_src + 4 : n_src + 4 + len(parts)], refs[n_src + 4 + len(parts) :]
    r = x_all.shape[1]

    @pl.when(pl.program_id(0) == 0)
    def _():
        at = 0
        for x_ref in x_refs:
            x_all[at : at + x_ref.shape[0]] = x_ref[...]
            at += x_ref.shape[0]
        for q in range(sum(parts)):
            hi, lo = split(x_all[idx_ref[q]] * keep_ref[...])
            rows = slice(q * r, (q + 1) * r)
            lh[rows, :] = hi[:, :cd]
            ll[rows, :] = lo[:, :cd]
            lt[rows, :] = jnp.concatenate([hi[:, cd:], hi[:, cd:], lo[:, cd:]], axis=1)

    dot = functools.partial(jnp.dot, preferred_element_type=jnp.float32)
    out = (
        dot(lh[...], hi_ref[...])
        + dot(lh[...], lo_ref[...])
        + dot(ll[...], hi_ref[...])
        + dot(lt[...], tail_ref[...])
    )
    at = 0
    for part, o_ref in zip(parts, outs):
        o_ref[...] = out[at * r : (at + part) * r]
        at += part


def product(idx, xs, r, keep, right, parts, tiles):
    hi, lo, tail = (pltpu.with_memory_space_constraint(x, pltpu.HBM) for x in right)
    cd, n = hi.shape
    k = keep.shape[1]
    xs = [x.reshape(-1, r, k) for x in xs]
    m = sum(parts) * r
    lo_tile, hi_tile = tiles
    width = min(hi_tile * TILE, n) - lo_tile * TILE
    col = lambda i, *_: (0, lo_tile + i)
    return pl.pallas_call(
        functools.partial(product_kernel, len(xs), cd, parts),
        grid_spec=pltpu.PrefetchScalarGridSpec(
            num_scalar_prefetch=1,
            grid=(hi_tile - lo_tile,),
            in_specs=[pl.BlockSpec(x.shape, lambda i, *_: (0, 0, 0)) for x in xs]
            + [
                pl.BlockSpec(keep.shape, lambda i, *_: (0, 0)),
                pl.BlockSpec((cd, TILE), col),
                pl.BlockSpec((cd, TILE), col),
                pl.BlockSpec((tail.shape[0], TILE), col),
            ],
            out_specs=[pl.BlockSpec((p * r, TILE), lambda i, *_: (0, i)) for p in parts],
            scratch_shapes=[
                pltpu.VMEM((NZ * NC, r, k), jnp.float32),
                pltpu.VMEM((m, cd), jnp.bfloat16),
                pltpu.VMEM((m, cd), jnp.bfloat16),
                pltpu.VMEM((m, tail.shape[0]), jnp.bfloat16),
            ],
        ),
        out_shape=[jax.ShapeDtypeStruct((p * r, width), jnp.float32) for p in parts],
        compiler_params=pltpu.CompilerParams(vmem_limit_bytes=32 << 20),
        cost_estimate=pl.CostEstimate(flops=COST, bytes_accessed=COST, transcendentals=0),
        name="product",
    )(idx, *xs, keep, hi, lo, tail)


def after(x, *deps):
    return lax.optimization_barrier((x, *deps))[0]


def ring_z(pair, right):
    r = pair.shape[0] // 2
    chain, back = [pair], []
    for step in range(3):
        chain.append(send(after(chain[-1], *right) if step == 1 else chain[-1], ALONG_Z))
        back.append(send(chain[-1], OTHER))
    far = send(chain[3][:r], ALONG_Z)
    return chain + [far] + back + [send(far, OTHER)]


def on_device(
    ladder_amps, vvvv_slice, cd_live, amplitudes, hole_inter, direct, occ_energy, vir_energy
):
    z, core = lax.axis_index("vr"), lax.axis_index("vc")
    mine = jnp.concatenate([ladder_amps, hole_inter], axis=1)
    live_cols = jnp.repeat(cd_live.astype(jnp.float32), BLOCK)
    keep = jnp.concatenate([live_cols, jnp.ones((hole_inter.shape[1],), jnp.float32)])[None, :]

    device = (lax.axis_index("occ") * NZ + z) * NC + core
    idx = lax.dynamic_slice_in_dim(jnp.asarray(places()), device, 1, 0)[0]
    n_first = sum(PARTS[:2])

    mine = send(mine, SLOTS)
    other = send(mine, OTHER)
    right = prepare(after(vvvv_slice, other), amplitudes)
    rounds, at = [], 0
    for r in SIZES:
        xs = ring_z(jnp.concatenate([mine[at : at + r], other[at : at + r]]), right)
        rounds += [(r, tiles, xs) for tiles in ROUNDS]
        at += r

    firsts, deps = [], ()
    for r, tiles, xs in rounds:
        s1p, s1m = product(after(idx[:n_first], *deps), xs, r, keep, right, PARTS[:2], tiles)
        firsts.append((send(s1p, first(1)), send(s1m, first(-1))))
        deps = (send(s1m[:8, :128], OTHER),)

    seconds = []
    for (r, tiles, xs), (r1p, r1m) in zip(rounds, firsts):
        mp, mm, own = deps = product(after(idx[n_first:], *deps), xs, r, keep, right, PARTS[2:], tiles)
        r2p, r2m = send(mp + r1p[: 2 * r], first(1)), send(mm + r1m[: 2 * r], first(-1))
        seconds.append((own[: 2 * r] + r2p + r1m[2 * r :], own[2 * r :] + r1p[2 * r :] + r2m))

    summed = []
    for (r, _, _), (g01, g23) in zip(rounds, seconds):
        h = r // 2
        t1p = jnp.concatenate([g23[:h], g01[r + h :]])
        t1m = jnp.concatenate([g23[h:r], g23[r : r + h]])
        u1p, u1m = send(t1p, second(1)), send(t1m, second(-1))
        u2p, u2m = send(g01[r : r + h] + u1p[:h], second(1)), send(g23[r + h :] + u1m[:h], second(-1))
        summed.append(jnp.concatenate([g01[:h] + u2p + u1m[h:], g01[h:r] + u1p[h:] + u2m]))
    n = len(ROUNDS)
    summed = [jnp.concatenate(summed[i : i + n], axis=1) for i in range(0, len(summed), n)]
    summed = jnp.concatenate(summed)
    return (direct + summed) / (vir_energy[None, :] - occ_energy[:, None])


def solution(mesh):
    in_specs = (
        P("occ", ("vr", "vc")),
        P("occ", ("vr", "vc")),
        P("occ"),
        P("occ", ("vr", "vc")),
        P("occ", ("vr", "vc")),
        P("occ", ("vr", "vc")),
        P("occ"),
        P(("vr", "vc")),
    )
    out_specs = P("occ", ("vr", "vc"))
    return jax.shard_map(
        on_device, mesh=mesh, in_specs=in_specs, out_specs=out_specs, check_vma=False
    )
```

time: 211 us -> 153 us (0.73)
  waiting for transfers between devices: 164 us -> 66.2 us
  Pallas kernels: 0 us -> 39.9 us
  starting transfers between devices: 1.96 us -> 40.6 us
  matrix products: 25 us -> 0 us
  between operations: 13.4 us -> 0.27 us
    reduce_scatter x1 -> x0, waiting for transfers between devices: 96.3 us -> none  [on_device(): summed = lax.psum_scatter(terms, 'occ', scatter_dimension=0, tiled=True)]
    all_gather x1 -> x0, waiting for transfers between devices: 63.6 us -> none  [on_device(): lax.all_gather(mine * keep[None, :], ('vr', 'vc'), axis=0, tiled=True)]
    ppermute x1 -> x26, waiting for transfers between devices: 4.6 us -> 66.2 us  [send(): return lax.ppermute(x, AXES, p)]
    pallas_call x0 -> x5, Pallas kernels: none -> 39.9 us  [the longest x4 30.6 us: product(): pl.pallas_call(functools.partial(product_kernel, len(xs), cd, parts), gri...]
    ppermute x1 -> x26, starting transfers between devices: 1.92 us -> 40.6 us  [send(): return lax.ppermute(x, AXES, p)]
    dot_general x1 -> x0, matrix products: 25 us -> none  [on_device(): jnp.dot(left, right, precision=lax.Precision.HIGH, preferred_element_type...]
  transfers between devices with their start and end apart: 3 -> 26, of which waited for: 3 -> 17; matrix products, arithmetic and copies ran while one was open for 0% -> 1% of each run, Pallas kernels for 0% -> 21%
where the time goes in v2:
time: 153 us; the launch traced here: 152 us
  waiting for transfers between devices  66.2 us (43%)
  starting transfers between devices  40.6 us (27%)
  Pallas kernels  39.9 us (26%)
  other arithmetic  3.38 us (2%)
  local copies, waits for them, and re-layouts  1.76 us (1%)
    ppermute x26, waiting for transfers between devices, send(): return lax.ppermute(x, AXES, p)  66.2 us
    ppermute x26, starting transfers between devices, send(): return lax.ppermute(x, AXES, p)  40.6 us
    pallas_call x4, Pallas kernels, product(): pl.pallas_call(functools.partial(product_kernel, len(xs), cd, parts), gri...  30.6 us
    pallas_call x1, Pallas kernels, prepare(): pl.pallas_call(prepare_kernel, grid=(pl.cdiv(n, TILE),), in_specs=[pl.Blo...  9.24 us
  transfers between devices with their start and end apart: 26, of which 17 were waited for; matrix products, arithmetic and copies ran while one was open for 1% of the time, Pallas kernels for 21%

profile of v2, /device:TPU:8, one launch (start us, length us, event | category | flops | bytes accessed | tf_op | source)
XLA Modules:
  0.0 152.0 jit_solution(16751308562309995847)
XLA Ops:
  0.0 1.0 pad_maximum_fusion.2
  1.0 7.1 %collective-permute-start = (f32[64,832]{1,0:T(8,128)S(1)}, f32[64,832]{1,0:T(8,128)S(1)}, u32[]{:S(2)}, u32[]{:S(2)}) collective-permute-start(f32[64,832]{1,0:T(8,128)S(1)} %pad_maximum_fusion.2), channel_id=1, source_target_pairs={{0,3},{1,29},{2,47},{3,53},{4,79},{5,89},{6,103},{7,115},{8,135},{... | collective-permute-start | bytes 638984 | tf_op jit(solution)/shard_map/ppermute | solution.py:87
  8.1 3.5 %collective-permute-done = f32[64,832]{1,0:T(8,128)S(1)} collective-permute-done((f32[64,832]{1,0:T(8,128)S(1)}, f32[64,832]{1,0:T(8,128)S(1)}, u32[]{:S(2)}, u32[]{:S(2)}) %collective-permute-start) | collective-permute-done | bytes 213024 | tf_op jit(solution)/shard_map/ppermute | solution.py:87
  11.7 3.4 %collective-permute-start.1 = (f32[64,832]{1,0:T(8,128)S(1)}, f32[64,832]{1,0:T(8,128)S(1)}, u32[]{:S(2)}, u32[]{:S(2)}) collective-permute-start(f32[64,832]{1,0:T(8,128)S(1)} %collective-permute-done), channel_id=1, source_target_pairs={{0,1},{1,0},{2,3},{3,2},{4,5},{5,4},{6,7},{7,6},{8,9},{9,8},{10,11... | collective-permute-start | bytes 638984 | tf_op jit(solution)/shard_map/ppermute | solution.py:87
  15.1 1.1 collective-permute-done.1
  16.3 3.0 %collective-permute-start.2 = (f32[128,832]{1,0:T(8,128)S(1)}, f32[128,832]{1,0:T(8,128)S(1)}, u32[]{:S(2)}, u32[]{:S(2)}) collective-permute-start(f32[128,832]{1,0:T(8,128)S(1)} %constant_dynamic-update-slice_fusion), channel_id=1, source_target_pairs={{0,2},{1,15},{2,4},{3,1},{4,6},{5,3},{6,8},{7,5},{8,10},{9,7},{10,... | collective-permute-start | bytes 1277960 | tf_op jit(solution)/shard_map/ppermute | solution.py:87
  19.2 9.2 %prepare.1 = (bf16[768,2944]{1,0:T(8,128)(2,1)}, bf16[768,2944]{1,0:T(8,128)(2,1)}, bf16[192,2944]{1,0:T(8,128)(2,1)}) custom-call(f32[768,2944]{1,0:T(8,128)} %v_ref, f32[64,2944]{1,0:T(8,128)S(1)} %copy-done), custom_call_target="tpu_custom_call" | custom-call | flops 9043968 | bytes 19595264 | tf_op jit(solution)/shard_map/prepare/pallas_call | solution.py:108
  28.5 11.3 %collective-permute-done.3 = f32[128,832]{1,0:T(8,128)S(1)} collective-permute-done((f32[128,832]{1,0:T(8,128)S(1)}, f32[128,832]{1,0:T(8,128)S(1)}, u32[]{:S(2)}, u32[]{:S(2)}) %collective-permute-start.3) | collective-permute-done | bytes 426016 | tf_op jit(solution)/shard_map/ppermute | solution.py:87
  39.8 9.7 %collective-permute-done.4 = f32[128,832]{1,0:T(8,128)S(1)} collective-permute-done((f32[128,832]{1,0:T(8,128)S(1)}, f32[128,832]{1,0:T(8,128)S(1)}, u32[]{:S(2)}, u32[]{:S(2)}) %collective-permute-start.4) | collective-permute-done | bytes 426016 | tf_op jit(solution)/shard_map/ppermute | solution.py:87
  49.5 0.7 slice.158
  50.2 0.7 collective-permute-start.5
  50.9 2.6 %collective-permute-start.6 = (f32[128,832]{1,0:T(8,128)S(1)}, f32[128,832]{1,0:T(8,128)S(1)}, u32[]{:S(2)}, u32[]{:S(2)}) collective-permute-start(f32[128,832]{1,0:T(8,128)S(1)} %collective-permute-done.2), channel_id=1, source_target_pairs={{0,1},{1,0},{2,3},{3,2},{4,5},{5,4},{6,7},{7,6},{8,9},{9,8},{10,11... | collective-permute-start | bytes 1277960 | tf_op jit(solution)/shard_map/ppermute | solution.py:87
  53.5 0.5 collective-permute-start.8
  54.0 0.7 constant_dynamic-slice_fusion
  54.7 2.9 %collective-permute-done.5 = f32[64,832]{1,0:T(8,128)S(1)} collective-permute-done((f32[64,832]{1,0:T(8,128)}, f32[64,832]{1,0:T(8,128)S(1)}, u32[]{:S(2)}, u32[]{:S(2)}) %collective-permute-start.5) | collective-permute-done | bytes 213024 | tf_op jit(solution)/shard_map/ppermute | solution.py:87
  57.9 1.4 collective-permute-done.9
  59.3 7.7 %product.7 = (f32[256,1408]{1,0:T(8,128)S(1)}, f32[256,1408]{1,0:T(8,128)S(1)}) custom-call(s32[8]{0:T(128)S(1)} %get-tuple-element.49.idx_ref, f32[2,64,832]{2,1,0:T(8,128)S(1)} %bitcast.17, f32[2,64,832]{2,1,0:T(8,128)S(1)} %bitcast.21, f32[2,64,832]{2,1,0:T(8,128)S(1)} %bitcast.25, f32[2,64,832]{2,1,0:T(8,128)S(1)} %bitcast.13, ...), custom_call_target="tpu_custom_call" | custom-call | flops 1000 | bytes 1000 | tf_op jit(solution)/shard_map/product/pallas_call | solution.py:164
  67.0 4.8 %collective-permute-start.20 = (f32[256,1408]{1,0:T(8,128)S(1)}, f32[256,1408]{1,0:T(8,128)S(1)}, u32[]{:S(2)}, u32[]{:S(2)}) collective-permute-start(f32[256,1408]{1,0:T(8,128)S(1)} %get-tuple-element.35), channel_id=1, source_target_pairs={{0,192},{1,49},{2,194},{3,51},{4,196},{5,53},{6,198},{7,55},{8,200... | collective-permute-start | bytes 4325384 | tf_op jit(solution)/shard_map/ppermute | solution.py:87
  71.8 7.5 %product.5 = (f32[256,1536]{1,0:T(8,128)S(1)}, f32[256,1536]{1,0:T(8,128)S(1)}) custom-call(s32[8]{0:T(128)S(1)} %get-tuple-element.49.idx_ref, f32[2,64,832]{2,1,0:T(8,128)S(1)} %bitcast.18, f32[2,64,832]{2,1,0:T(8,128)S(1)} %bitcast.22, f32[2,64,832]{2,1,0:T(8,128)S(1)} %bitcast.26, f32[2,64,832]{2,1,0:T(8,128)S(1)} %bitcast.14, ...), custom_call_target="tpu_custom_call" | custom-call | flops 1000 | bytes 1000 | tf_op jit(solution)/shard_map/product/pallas_call | solution.py:164
  79.3 3.5 %collective-permute-start.12 = (f32[256,1536]{1,0:T(8,128)S(1)}, f32[256,1536]{1,0:T(8,128)S(1)}, u32[]{:S(2)}, u32[]{:S(2)}) collective-permute-start(f32[256,1536]{1,0:T(8,128)S(1)} %get-tuple-element.29), channel_id=1, source_target_pairs={{0,192},{1,49},{2,194},{3,51},{4,196},{5,53},{6,198},{7,55},{8,200... | collective-permute-start | bytes 4718600 | tf_op jit(solution)/shard_map/ppermute | solution.py:87
  82.8 7.5 %product.4 = (f32[128,1536]{1,0:T(8,128)S(1)}, f32[128,1536]{1,0:T(8,128)S(1)}, f32[256,1536]{1,0:T(8,128)S(1)}) custom-call(s32[8]{0:T(128)S(1)} %get-tuple-element.31.idx_ref, f32[2,64,832]{2,1,0:T(8,128)S(1)} %bitcast.19, f32[2,64,832]{2,1,0:T(8,128)S(1)} %bitcast.23, f32[2,64,832]{2,1,0:T(8,128)S(1)} %bitcast.27, f32[2,64,832]{2,1,0:T(8,128)S(1)} %bitcast.15, ...), custom_call_target="tpu_custom_call" | custom-call | flops 1000 | bytes 1000 | tf_op jit(solution)/shard_map/product/pallas_call | solution.py:164
  90.4 0.1 collective-permute-start.10
  90.5 7.8 %product.6 = (f32[128,1408]{1,0:T(8,128)S(1)}, f32[128,1408]{1,0:T(8,128)S(1)}, f32[256,1408]{1,0:T(8,128)S(1)}) custom-call(s32[8]{0:T(128)S(1)} %get-tuple-element.31.idx_ref, f32[2,64,832]{2,1,0:T(8,128)S(1)} %bitcast.20, f32[2,64,832]{2,1,0:T(8,128)S(1)} %bitcast.24, f32[2,64,832]{2,1,0:T(8,128)S(1)} %bitcast.28, f32[2,64,832]{2,1,0:T(8,128)S(1)} %bitcast.16, ...), custom_call_target="tpu_custom_call" | custom-call | flops 1000 | bytes 1000 | tf_op jit(solution)/shard_map/product/pallas_call | solution.py:164
  98.4 3.3 %collective-permute-start.21 = (f32[128,1408]{1,0:T(8,128)S(1)}, f32[128,1408]{1,0:T(8,128)S(1)}, u32[]{:S(2)}, u32[]{:S(2)}) collective-permute-start(f32[128,1408]{1,0:T(8,128)S(1)} %slice_add_fusion.4), channel_id=1, source_target_pairs={{0,192},{1,49},{2,194},{3,51},{4,196},{5,53},{6,198},{7,55},{8,200... | collective-permute-start | bytes 2162696 | tf_op jit(solution)/shard_map/ppermute | solution.py:87
  101.9 3.3 %collective-permute-done.12 = f32[256,1536]{1,0:T(8,128)S(1)} collective-permute-done((f32[256,1536]{1,0:T(8,128)S(1)}, f32[256,1536]{1,0:T(8,128)S(1)}, u32[]{:S(2)}, u32[]{:S(2)}) %collective-permute-start.12) | collective-permute-done | bytes 1572896 | tf_op jit(solution)/shard_map/ppermute | solution.py:87
  105.2 0.1 slice_add_fusion
  105.3 3.8 %collective-permute-start.13 = (f32[128,1536]{1,0:T(8,128)S(1)}, f32[128,1536]{1,0:T(8,128)S(1)}, u32[]{:S(2)}, u32[]{:S(2)}) collective-permute-start(f32[128,1536]{1,0:T(8,128)S(1)} %slice_add_fusion), channel_id=1, source_target_pairs={{0,192},{1,49},{2,194},{3,51},{4,196},{5,53},{6,198},{7,55},{8,200... | collective-permute-start | bytes 2359304 | tf_op jit(solution)/shard_map/ppermute | solution.py:87
  109.0 3.0 %collective-permute-done.10 = f32[256,1536]{1,0:T(8,128)S(1)} collective-permute-done((f32[256,1536]{1,0:T(8,128)S(1)}, f32[256,1536]{1,0:T(8,128)S(1)}, u32[]{:S(2)}, u32[]{:S(2)}) %collective-permute-start.10) | collective-permute-done | bytes 1572896 | tf_op jit(solution)/shard_map/ppermute | solution.py:87
  112.1 0.1 slice_add_fusion.3
  112.3 0.6 collective-permute-done.21
  112.9 6.9 %collective-permute-done.19 = f32[128,1408]{1,0:T(8,128)S(1)} collective-permute-done((f32[128,1408]{1,0:T(8,128)S(1)}, f32[128,1408]{1,0:T(8,128)S(1)}, u32[]{:S(2)}, u32[]{:S(2)}) %collective-permute-start.19) | collective-permute-done | bytes 720928 | tf_op jit(solution)/shard_map/ppermute | solution.py:87
  119.8 0.2 slice_add_fusion.6
  120.1 1.5 %collective-permute-start.24 = (f32[64,1408]{1,0:T(8,128)S(1)}, f32[64,1408]{1,0:T(8,128)S(1)}, u32[]{:S(2)}, u32[]{:S(2)}) collective-permute-start(f32[64,1408]{1,0:T(8,128)S(1)} %concatenate.41), channel_id=1, source_target_pairs={{0,48},{1,193},{2,50},{3,195},{4,52},{5,197},{6,54},{7,199},{8,56}... | collective-permute-start | bytes 1081352 | tf_op jit(solution)/shard_map/ppermute | solution.py:87
  121.6 3.2 %collective-permute-done.13 = f32[128,1536]{1,0:T(8,128)S(1)} collective-permute-done((f32[128,1536]{1,0:T(8,128)S(1)}, f32[128,1536]{1,0:T(8,128)S(1)}, u32[]{:S(2)}, u32[]{:S(2)}) %collective-permute-start.13) | collective-permute-done | bytes 786464 | tf_op jit(solution)/shard_map/ppermute | solution.py:87
  124.8 3.4 %collective-permute-done.11 = f32[128,1536]{1,0:T(8,128)S(1)} collective-permute-done((f32[128,1536]{1,0:T(8,128)S(1)}, f32[128,1536]{1,0:T(8,128)S(1)}, u32[]{:S(2)}, u32[]{:S(2)}) %collective-permute-start.11) | collective-permute-done | bytes 786464 | tf_op jit(solution)/shard_map/ppermute | solution.py:87
  128.2 0.4 slice_add_fusion.2
  128.7 1.5 %collective-permute-start.16 = (f32[64,1536]{1,0:T(8,128)S(1)}, f32[64,1536]{1,0:T(8,128)S(1)}, u32[]{:S(2)}, u32[]{:S(2)}) collective-permute-start(f32[64,1536]{1,0:T(8,128)S(1)} %concatenate.40), channel_id=1, source_target_pairs={{0,48},{1,193},{2,50},{3,195},{4,52},{5,197},{6,54},{7,199},{8,56}... | collective-permute-start | bytes 1179656 | tf_op jit(solution)/shard_map/ppermute | solution.py:87
  130.3 0.6 collective-permute-start.22
  130.9 1.5 collective-permute-start.25
  132.4 4.1 %collective-permute-done.16 = f32[64,1536]{1,0:T(8,128)S(1)} collective-permute-done((f32[64,1536]{1,0:T(8,128)S(1)}, f32[64,1536]{1,0:T(8,128)S(1)}, u32[]{:S(2)}, u32[]{:S(2)}) %collective-permute-start.16) | collective-permute-done | bytes 393248 | tf_op jit(solution)/shard_map/ppermute | solution.py:87
  136.7 2.0 %collective-permute-start.17 = (f32[32,1536]{1,0:T(8,128)S(1)}, f32[32,1536]{1,0:T(8,128)S(1)}, u32[]{:S(2)}, u32[]{:S(2)}) collective-permute-start(f32[32,1536]{1,0:T(8,128)S(1)} %get-tuple-element.46), channel_id=1, source_target_pairs={{0,48},{1,193},{2,50},{3,195},{4,52},{5,197},{6,54},{7,199},{8,56}... | collective-permute-start | bytes 589832 | tf_op jit(solution)/shard_map/ppermute | solution.py:87
  138.8 0.2 collective-permute-start.23
  139.0 3.5 %collective-permute-done.17 = f32[32,1536]{1,0:T(8,128)S(1)} collective-permute-done((f32[32,1536]{1,0:T(8,128)S(1)}, f32[32,1536]{1,0:T(8,128)S(1)}, u32[]{:S(2)}, u32[]{:S(2)}) %collective-permute-start.17) | collective-permute-done | bytes 196640 | tf_op jit(solution)/shard_map/ppermute | solution.py:87
  142.5 2.0 %collective-permute-done.14 = f32[64,1536]{1,0:T(8,128)S(1)} collective-permute-done((f32[64,1536]{1,0:T(8,128)S(1)}, f32[64,1536]{1,0:T(8,128)S(1)}, u32[]{:S(2)}, u32[]{:S(2)}) %collective-permute-start.14) | collective-permute-done | bytes 393248 | tf_op jit(solution)/shard_map/ppermute | solution.py:87
  144.5 0.1 collective-permute-start.15
  144.6 1.7 %collective-permute-done.23 = f32[32,1408]{1,0:T(8,128)S(1)} collective-permute-done((f32[32,1408]{1,0:T(8,128)S(1)}, f32[32,1408]{1,0:T(8,128)S(1)}, u32[]{:S(2)}, u32[]{:S(2)}) %collective-permute-start.23) | collective-permute-done | bytes 180256 | tf_op jit(solution)/shard_map/ppermute | solution.py:87
  146.4 4.5 %collective-permute-done.15 = f32[32,1536]{1,0:T(8,128)S(1)} collective-permute-done((f32[32,1536]{1,0:T(8,128)S(1)}, f32[32,1536]{1,0:T(8,128)S(1)}, u32[]{:S(2)}, u32[]{:S(2)}) %collective-permute-start.15) | collective-permute-done | bytes 196640 | tf_op jit(solution)/shard_map/ppermute | solution.py:87
  151.0 1.0 fusion.1
  (49 shorter events, 1.2 us)
Async XLA Ops:
  0.0 19.2 %copy-start = (f32[64,2944]{1,0:T(8,128)S(1)}, f32[64,2944]{1,0:T(8,128)}, u32[]{:S(2)}) copy-start(f32[64,2944]{1,0:T(8,128)} %a_ref.1) | copy-start | bytes 2260996
  1.0 10.6 %collective-permute-start = (f32[64,832]{1,0:T(8,128)S(1)}, f32[64,832]{1,0:T(8,128)S(1)}, u32[]{:S(2)}, u32[]{:S(2)}) collective-permute-start(f32[64,832]{1,0:T(8,128)S(1)} %pad_maximum_fusion.2), channel_id=1, source_target_pairs={{0,3},{1,29},{2,47},{3,53},{4,79},{5,89},{6,103},{7,115},{8,135},{... | collective-permute-start | bytes 638984 | tf_op jit(solution)/shard_map/ppermute | solution.py:87
  11.7 4.6 %collective-permute-start.1 = (f32[64,832]{1,0:T(8,128)S(1)}, f32[64,832]{1,0:T(8,128)S(1)}, u32[]{:S(2)}, u32[]{:S(2)}) collective-permute-start(f32[64,832]{1,0:T(8,128)S(1)} %collective-permute-done), channel_id=1, source_target_pairs={{0,1},{1,0},{2,3},{3,2},{4,5},{5,4},{6,7},{7,6},{8,9},{9,8},{10,11... | collective-permute-start | bytes 638984 | tf_op jit(solution)/shard_map/ppermute | solution.py:87
  16.2 41.5 %copy-start.4 = (s32[12]{0:T(128)S(1)}, s32[12]{0:T(128)}, u32[]{:S(2)}) copy-start(s32[12]{0:T(128)} %param.11) | copy-start | bytes 148
  16.3 12.2 %collective-permute-start.2 = (f32[128,832]{1,0:T(8,128)S(1)}, f32[128,832]{1,0:T(8,128)S(1)}, u32[]{:S(2)}, u32[]{:S(2)}) collective-permute-start(f32[128,832]{1,0:T(8,128)S(1)} %constant_dynamic-update-slice_fusion), channel_id=1, source_target_pairs={{0,2},{1,15},{2,4},{3,1},{4,6},{5,3},{6,8},{7,5},{8,10},{9,7},{10,... | collective-permute-start | bytes 1277960 | tf_op jit(solution)/shard_map/ppermute | solution.py:87
  28.5 11.3 %collective-permute-start.3 = (f32[128,832]{1,0:T(8,128)S(1)}, f32[128,832]{1,0:T(8,128)S(1)}, u32[]{:S(2)}, u32[]{:S(2)}) collective-permute-start(f32[128,832]{1,0:T(8,128)S(1)} %collective-permute-done.2), channel_id=1, source_target_pairs={{0,2},{1,15},{2,4},{3,1},{4,6},{5,3},{6,8},{7,5},{8,10},{9,7},{10,... | collective-permute-start | bytes 1277960 | tf_op jit(solution)/shard_map/ppermute | solution.py:87
  39.8 9.7 %collective-permute-start.4 = (f32[128,832]{1,0:T(8,128)S(1)}, f32[128,832]{1,0:T(8,128)S(1)}, u32[]{:S(2)}, u32[]{:S(2)}) collective-permute-start(f32[128,832]{1,0:T(8,128)S(1)} %collective-permute-done.3), channel_id=1, source_target_pairs={{0,2},{1,15},{2,4},{3,1},{4,6},{5,3},{6,8},{7,5},{8,10},{9,7},{10,... | collective-permute-start | bytes 1277960 | tf_op jit(solution)/shard_map/ppermute | solution.py:87
  50.2 7.4 %collective-permute-start.5 = (f32[64,832]{1,0:T(8,128)}, f32[64,832]{1,0:T(8,128)S(1)}, u32[]{:S(2)}, u32[]{:S(2)}) collective-permute-start(f32[64,832]{1,0:T(8,128)} %slice.158), channel_id=1, source_target_pairs={{0,2},{1,15},{2,4},{3,1},{4,6},{5,3},{6,8},{7,5},{8,10},{9,7},{10,... | collective-permute-start | bytes 638984 | tf_op jit(solution)/shard_map/ppermute | solution.py:87
  50.9 7.0 %collective-permute-start.6 = (f32[128,832]{1,0:T(8,128)S(1)}, f32[128,832]{1,0:T(8,128)S(1)}, u32[]{:S(2)}, u32[]{:S(2)}) collective-permute-start(f32[128,832]{1,0:T(8,128)S(1)} %collective-permute-done.2), channel_id=1, source_target_pairs={{0,1},{1,0},{2,3},{3,2},{4,5},{5,4},{6,7},{7,6},{8,9},{9,8},{10,11... | collective-permute-start | bytes 1277960 | tf_op jit(solution)/shard_map/ppermute | solution.py:87
  53.5 4.4 %collective-permute-start.7 = (f32[128,832]{1,0:T(8,128)S(1)}, f32[128,832]{1,0:T(8,128)S(1)}, u32[]{:S(2)}, u32[]{:S(2)}) collective-permute-start(f32[128,832]{1,0:T(8,128)S(1)} %collective-permute-done.3), channel_id=1, source_target_pairs={{0,1},{1,0},{2,3},{3,2},{4,5},{5,4},{6,7},{7,6},{8,9},{9,8},{10,11... | collective-permute-start | bytes 1277960 | tf_op jit(solution)/shard_map/ppermute | solution.py:87
  53.5 5.8 %collective-permute-start.8 = (f32[128,832]{1,0:T(8,128)S(1)}, f32[128,832]{1,0:T(8,128)S(1)}, u32[]{:S(2)}, u32[]{:S(2)}) collective-permute-start(f32[128,832]{1,0:T(8,128)S(1)} %collective-permute-done.4), channel_id=1, source_target_pairs={{0,1},{1,0},{2,3},{3,2},{4,5},{5,4},{6,7},{7,6},{8,9},{9,8},{10,11... | collective-permute-start | bytes 1277960 | tf_op jit(solution)/shard_map/ppermute | solution.py:87
  57.6 1.6 %collective-permute-start.9 = (f32[64,832]{1,0:T(8,128)S(1)}, f32[64,832]{1,0:T(8,128)}, u32[]{:S(2)}, u32[]{:S(2)}) collective-permute-start(f32[64,832]{1,0:T(8,128)S(1)} %collective-permute-done.5), channel_id=1, source_target_pairs={{0,1},{1,0},{2,3},{3,2},{4,5},{5,4},{6,7},{7,6},{8,9},{9,8},{10,11... | collective-permute-start | bytes 638984 | tf_op jit(solution)/shard_map/ppermute | solution.py:87
  67.0 31.3 %collective-permute-start.20 = (f32[256,1408]{1,0:T(8,128)S(1)}, f32[256,1408]{1,0:T(8,128)S(1)}, u32[]{:S(2)}, u32[]{:S(2)}) collective-permute-start(f32[256,1408]{1,0:T(8,128)S(1)} %get-tuple-element.35), channel_id=1, source_target_pairs={{0,192},{1,49},{2,194},{3,51},{4,196},{5,53},{6,198},{7,55},{8,200... | collective-permute-start | bytes 4325384 | tf_op jit(solution)/shard_map/ppermute | solution.py:87
  71.8 29.9 %collective-permute-start.18 = (f32[256,1408]{1,0:T(8,128)S(1)}, f32[256,1408]{1,0:T(8,128)S(1)}, u32[]{:S(2)}, u32[]{:S(2)}) collective-permute-start(f32[256,1408]{1,0:T(8,128)S(1)} %get-tuple-element.34), channel_id=1, source_target_pairs={{0,64},{1,17},{2,66},{3,19},{4,68},{5,21},{6,70},{7,23},{8,72},{9,... | collective-permute-start | bytes 4325384 | tf_op jit(solution)/shard_map/ppermute | solution.py:87
  79.3 25.8 %collective-permute-start.12 = (f32[256,1536]{1,0:T(8,128)S(1)}, f32[256,1536]{1,0:T(8,128)S(1)}, u32[]{:S(2)}, u32[]{:S(2)}) collective-permute-start(f32[256,1536]{1,0:T(8,128)S(1)} %get-tuple-element.29), channel_id=1, source_target_pairs={{0,192},{1,49},{2,194},{3,51},{4,196},{5,53},{6,198},{7,55},{8,200... | collective-permute-start | bytes 4718600 | tf_op jit(solution)/shard_map/ppermute | solution.py:87
  90.4 21.7 %collective-permute-start.10 = (f32[256,1536]{1,0:T(8,128)S(1)}, f32[256,1536]{1,0:T(8,128)S(1)}, u32[]{:S(2)}, u32[]{:S(2)}) collective-permute-start(f32[256,1536]{1,0:T(8,128)S(1)} %get-tuple-element.28), channel_id=1, source_target_pairs={{0,64},{1,17},{2,66},{3,19},{4,68},{5,21},{6,70},{7,23},{8,72},{9,... | collective-permute-start | bytes 4718600 | tf_op jit(solution)/shard_map/ppermute | solution.py:87
  98.4 14.5 %collective-permute-start.21 = (f32[128,1408]{1,0:T(8,128)S(1)}, f32[128,1408]{1,0:T(8,128)S(1)}, u32[]{:S(2)}, u32[]{:S(2)}) collective-permute-start(f32[128,1408]{1,0:T(8,128)S(1)} %slice_add_fusion.4), channel_id=1, source_target_pairs={{0,192},{1,49},{2,194},{3,51},{4,196},{5,53},{6,198},{7,55},{8,200... | collective-permute-start | bytes 2162696 | tf_op jit(solution)/shard_map/ppermute | solution.py:87
  101.8 18.0 %collective-permute-start.19 = (f32[128,1408]{1,0:T(8,128)S(1)}, f32[128,1408]{1,0:T(8,128)S(1)}, u32[]{:S(2)}, u32[]{:S(2)}) collective-permute-start(f32[128,1408]{1,0:T(8,128)S(1)} %slice_add_fusion.7), channel_id=1, source_target_pairs={{0,64},{1,17},{2,66},{3,19},{4,68},{5,21},{6,70},{7,23},{8,72},{9,... | collective-permute-start | bytes 2162696 | tf_op jit(solution)/shard_map/ppermute | solution.py:87
  105.3 19.6 %collective-permute-start.13 = (f32[128,1536]{1,0:T(8,128)S(1)}, f32[128,1536]{1,0:T(8,128)S(1)}, u32[]{:S(2)}, u32[]{:S(2)}) collective-permute-start(f32[128,1536]{1,0:T(8,128)S(1)} %slice_add_fusion), channel_id=1, source_target_pairs={{0,192},{1,49},{2,194},{3,51},{4,196},{5,53},{6,198},{7,55},{8,200... | collective-permute-start | bytes 2359304 | tf_op jit(solution)/shard_map/ppermute | solution.py:87
  112.2 16.1 %collective-permute-start.11 = (f32[128,1536]{1,0:T(8,128)S(1)}, f32[128,1536]{1,0:T(8,128)S(1)}, u32[]{:S(2)}, u32[]{:S(2)}) collective-permute-start(f32[128,1536]{1,0:T(8,128)S(1)} %slice_add_fusion.3), channel_id=1, source_target_pairs={{0,64},{1,17},{2,66},{3,19},{4,68},{5,21},{6,70},{7,23},{8,72},{9,... | collective-permute-start | bytes 2359304 | tf_op jit(solution)/shard_map/ppermute | solution.py:87
  120.1 10.2 %collective-permute-start.24 = (f32[64,1408]{1,0:T(8,128)S(1)}, f32[64,1408]{1,0:T(8,128)S(1)}, u32[]{:S(2)}, u32[]{:S(2)}) collective-permute-start(f32[64,1408]{1,0:T(8,128)S(1)} %concatenate.41), channel_id=1, source_target_pairs={{0,48},{1,193},{2,50},{3,195},{4,52},{5,197},{6,54},{7,199},{8,56}... | collective-permute-start | bytes 1081352 | tf_op jit(solution)/shard_map/ppermute | solution.py:87
  128.7 7.9 %collective-permute-start.16 = (f32[64,1536]{1,0:T(8,128)S(1)}, f32[64,1536]{1,0:T(8,128)S(1)}, u32[]{:S(2)}, u32[]{:S(2)}) collective-permute-start(f32[64,1536]{1,0:T(8,128)S(1)} %concatenate.40), channel_id=1, source_target_pairs={{0,48},{1,193},{2,50},{3,195},{4,52},{5,197},{6,54},{7,199},{8,56}... | collective-permute-start | bytes 1179656 | tf_op jit(solution)/shard_map/ppermute | solution.py:87
  130.3 8.4 %collective-permute-start.22 = (f32[64,1408]{1,0:T(8,128)S(1)}, f32[64,1408]{1,0:T(8,128)S(1)}, u32[]{:S(2)}, u32[]{:S(2)}) collective-permute-start(f32[64,1408]{1,0:T(8,128)S(1)} %pad_maximum_fusion.1), channel_id=1, source_target_pairs={{0,16},{1,65},{2,18},{3,67},{4,20},{5,69},{6,22},{7,71},{8,24},{9,... | collective-permute-start | bytes 1081352 | tf_op jit(solution)/shard_map/ppermute | solution.py:87
  130.9 7.8 %collective-permute-start.25 = (f32[32,1408]{1,0:T(8,128)S(1)}, f32[32,1408]{1,0:T(8,128)S(1)}, u32[]{:S(2)}, u32[]{:S(2)}) collective-permute-start(f32[32,1408]{1,0:T(8,128)S(1)} %get-tuple-element.48), channel_id=1, source_target_pairs={{0,48},{1,193},{2,50},{3,195},{4,52},{5,197},{6,54},{7,199},{8,56}... | collective-permute-start | bytes 540680 | tf_op jit(solution)/shard_map/ppermute | solution.py:87
  136.6 7.9 %collective-permute-start.14 = (f32[64,1536]{1,0:T(8,128)S(1)}, f32[64,1536]{1,0:T(8,128)S(1)}, u32[]{:S(2)}, u32[]{:S(2)}) collective-permute-start(f32[64,1536]{1,0:T(8,128)S(1)} %pad_maximum_fusion), channel_id=1, source_target_pairs={{0,16},{1,65},{2,18},{3,67},{4,20},{5,69},{6,22},{7,71},{8,24},{9,... | collective-permute-start | bytes 1179656 | tf_op jit(solution)/shard_map/ppermute | solution.py:87
  136.7 5.8 %collective-permute-start.17 = (f32[32,1536]{1,0:T(8,128)S(1)}, f32[32,1536]{1,0:T(8,128)S(1)}, u32[]{:S(2)}, u32[]{:S(2)}) collective-permute-start(f32[32,1536]{1,0:T(8,128)S(1)} %get-tuple-element.46), channel_id=1, source_target_pairs={{0,48},{1,193},{2,50},{3,195},{4,52},{5,197},{6,54},{7,199},{8,56}... | collective-permute-start | bytes 589832 | tf_op jit(solution)/shard_map/ppermute | solution.py:87
  138.8 12.2 %copy-start.1 = (f32[64,2944]{1,0:T(8,128)S(1)}, f32[64,2944]{1,0:T(8,128)}, u32[]{:S(2)}) copy-start(f32[64,2944]{1,0:T(8,128)} %param.14) | copy-start | bytes 2260996
  138.8 12.2 %copy-start.2 = (f32[2944]{0:T(1024)S(1)}, f32[2944]{0:T(1024)}, u32[]{:S(2)}) copy-start(f32[2944]{0:T(1024)} %param.16) | copy-start | bytes 35332
  138.8 12.2 %copy-start.3 = (f32[64]{0:T(128)S(1)}, f32[64]{0:T(128)}, u32[]{:S(2)}) copy-start(f32[64]{0:T(128)} %param.15) | copy-start | bytes 772
  138.8 7.6 %collective-permute-start.23 = (f32[32,1408]{1,0:T(8,128)S(1)}, f32[32,1408]{1,0:T(8,128)S(1)}, u32[]{:S(2)}, u32[]{:S(2)}) collective-permute-start(f32[32,1408]{1,0:T(8,128)S(1)} %get-tuple-element.43), channel_id=1, source_target_pairs={{0,16},{1,65},{2,18},{3,67},{4,20},{5,69},{6,22},{7,71},{8,24},{9,... | collective-permute-start | bytes 540680 | tf_op jit(solution)/shard_map/ppermute | solution.py:87
  144.5 6.4 %collective-permute-start.15 = (f32[32,1536]{1,0:T(8,128)S(1)}, f32[32,1536]{1,0:T(8,128)S(1)}, u32[]{:S(2)}, u32[]{:S(2)}) collective-permute-start(f32[32,1536]{1,0:T(8,128)S(1)} %get-tuple-element.41), channel_id=1, source_target_pairs={{0,16},{1,65},{2,18},{3,67},{4,20},{5,69},{6,22},{7,71},{8,24},{9,... | collective-permute-start | bytes 589832 | tf_op jit(solution)/shard_map/ppermute | solution.py:87

commit v3 on v2

v3 whole, which is shorter than its diff:
```python
import functools

import jax
import jax.numpy as jnp
import numpy as np
from jax import lax
from jax.experimental import pallas as pl
from jax.experimental.pallas import tpu as pltpu
from jax.sharding import PartitionSpec as P

BLOCK = 64
AXES = ("occ", "vr", "vc")
NX, NY, NZ, NC = 4, 4, 8, 2
TILE = 512
COST = 1000
STREAMS = 2
ROUNDS = ((0, 3), (3, 6))
ORDER = (
    (2, 0), (2, 1), (1, 2), (1, 3),
    (2, 2), (2, 3), (3, 0), (3, 1),
    (1, 0), (1, 1),
    (3, 2), (3, 3),
    (0, 0), (0, 1), (0, 2), (0, 3),
)
PARTS = (4, 4, 2, 2, 4)


def place(x, y, z, k):
    return (((x % NX) * NY + y % NY) * NZ + z % NZ) * NC + k % NC


def pairs(fn):
    out = []
    for x in range(NX):
        for y in range(NY):
            for z in range(NZ):
                for k in range(NC):
                    out.append((place(x, y, z, k), place(*fn(x, y, z, k))))
    return out


def first(d):
    return pairs(lambda x, y, z, k: (x + d, y, z, k) if k == 0 else (x, y + d, z, k))


def second(d):
    return pairs(lambda x, y, z, k: (x, y + d, z, k) if k == 0 else (x + d, y, z, k))


FROM = (6, 3, 4, 7, 4, 1, 0, 6, 0, 4, 6, 2, 3, 7, 1, 5)
TO = (3, 1, 0, 2, 2, 4, 7, 6, 1, 6, 0, 5, 7, 5, 3, 4)
CORE = (1, 1, 0, 1, 0, 1, 0, 0, 0, 1, 1, 1, 1, 0, 0, 0)


def to_slots(x, y, z, k):
    c, o = z * NC + k, x * NY + y
    return c // NY, c % NY, FROM[c] + TO[o], CORE[o]


def places():
    table = np.zeros((NX * NY * NZ * NC, len(ORDER)), np.int32)
    for x in range(NX):
        for y in range(NY):
            for z in range(NZ):
                for k in range(NC):
                    for q, (a, b) in enumerate(ORDER):
                        o = (x + a) % NX * NY + (y + b) % NY if k == 0 else (x + b) % NX * NY + (y + a) % NY
                        home = FROM[x * NY + y] + TO[o]
                        steps = (z - home if k == 0 else home - z) % NZ
                        other = int(CORE[o] != k)
                        if steps < 4:
                            at = 2 * steps + other
                        elif steps == 4:
                            at = 15 if other else 8
                        else:
                            at = 9 + 2 * (NZ - 1 - steps) + 1 - other
                        table[place(x, y, z, k), q] = at
    return table


SLOTS = pairs(to_slots)
ALONG_Z = pairs(lambda x, y, z, k: (x, y, z + (1 if k == 0 else -1), k))
OTHER = pairs(lambda x, y, z, k: (x, y, z, 1 - k))


def send(x, p):
    return lax.ppermute(x, AXES, p)


def split(x):
    hi = x.astype(jnp.bfloat16)
    return hi, (x - hi.astype(jnp.float32)).astype(jnp.bfloat16)


def product_kernel(n_src, n_deps, cd, parts, given, idx_ref, live_ref, *refs):
    x_refs, right_refs = refs[:n_src], refs[n_src : n_src + (3 if given else 2)]
    refs = refs[n_src + len(right_refs) + n_deps :]
    outs, refs = refs[: len(parts)], refs[len(parts) :]
    x_all, lh, ll, lt = refs[-4:]
    if given:
        hi_ref, lo_ref, tail_ref = right_refs
    else:
        hi_ref, lo_ref, tail_ref = refs[:3]
        hi_ref[...], lo_ref[...] = split(right_refs[0][...])
        ah, al = split(right_refs[1][...])
        tail_ref[...] = jnp.concatenate([ah, al, ah], axis=0)
    r = x_all.shape[2]

    @pl.when(pl.program_id(0) == 0)
    def _():
        column = lax.broadcasted_iota(jnp.int32, (1, x_all.shape[3]), 1)
        keep = jnp.ones(column.shape, jnp.float32)
        for i in range(cd // BLOCK):
            inside = (column >= i * BLOCK) & (column < (i + 1) * BLOCK)
            keep = jnp.where(inside, live_ref[i].astype(jnp.float32), keep)
        at = 0
        for i in range(0, 5 * STREAMS, STREAMS):
            here = x_refs[i].shape[0]
            for s in range(STREAMS):
                x_all[s, at : at + here] = x_refs[i + s][...]
            at += here
        for x_ref in x_refs[5 * STREAMS :]:
            here = x_ref.shape[0] // STREAMS
            for s in range(STREAMS):
                x_all[s, at : at + here] = x_ref[s * here : (s + 1) * here]
            at += here
        for q in range(sum(parts)):
            for s in range(STREAMS):
                hi, lo = split(x_all[s, idx_ref[q]] * keep)
                rows = slice((q * STREAMS + s) * r, (q * STREAMS + s + 1) * r)
                lh[rows, :] = hi[:, :cd]
                ll[rows, :] = lo[:, :cd]
                lt[rows, :] = jnp.concatenate([hi[:, cd:], hi[:, cd:], lo[:, cd:]], axis=1)

    r *= STREAMS
    dot = functools.partial(jnp.dot, preferred_element_type=jnp.float32)
    out = (
        dot(lh[...], hi_ref[...])
        + dot(lh[...], lo_ref[...])
        + dot(ll[...], hi_ref[...])
        + dot(lt[...], tail_ref[...])
    )
    at = 0
    for part, o_ref in zip(parts, outs):
        o_ref[...] = out[at * r : (at + part) * r]
        at += part


def product(idx, live, xs, r, right, parts, tiles=None, deps=()):
    k = xs[0].shape[1]
    xs = [x.reshape(-1, r // STREAMS, k) for x in xs]
    m = sum(parts) * r
    cd = right[0].shape[0]
    o = k - cd
    col = lambda i, *_: (0, i)
    if tiles:
        right = [pltpu.with_memory_space_constraint(x, pltpu.HBM) for x in right]
        n = min(tiles[1] * TILE, right[0].shape[1]) - tiles[0] * TILE
        source = lambda i, *_: (0, tiles[0] + i)
        right_specs = [pl.BlockSpec((cd, TILE), source), pl.BlockSpec((o, TILE), source)]
        heights = (cd, cd, 3 * o)
    else:
        right = [pltpu.with_memory_space_constraint(x, pltpu.HBM) for x in right]
        n = right[0].shape[1]
        right_specs = [pl.BlockSpec((x.shape[0], TILE), col) for x in right]
        heights = ()
    out = pl.pallas_call(
        functools.partial(product_kernel, len(xs), len(deps), cd, parts, not tiles),
        grid_spec=pltpu.PrefetchScalarGridSpec(
            num_scalar_prefetch=2,
            grid=(pl.cdiv(n, TILE),),
            in_specs=[pl.BlockSpec(x.shape, lambda i, *_: (0, 0, 0)) for x in xs]
            + right_specs
            + [pl.BlockSpec(memory_space=pl.ANY)] * len(deps),
            out_specs=[pl.BlockSpec((p * r, TILE), col) for p in parts]
            + [pl.BlockSpec((h, TILE), col) for h in heights],
            scratch_shapes=[
                pltpu.VMEM((STREAMS, NZ * NC, r // STREAMS, k), jnp.float32),
                pltpu.VMEM((m, cd), jnp.bfloat16),
                pltpu.VMEM((m, cd), jnp.bfloat16),
                pltpu.VMEM((m, 3 * o), jnp.bfloat16),
            ],
        ),
        out_shape=[jax.ShapeDtypeStruct((p * r, n), jnp.float32) for p in parts]
        + [pltpu.HBM((h, n), jnp.bfloat16) for h in heights],
        compiler_params=pltpu.CompilerParams(vmem_limit_bytes=36 << 20),
        cost_estimate=pl.CostEstimate(flops=COST, bytes_accessed=COST, transcendentals=0),
        name="product",
    )(idx, live, *xs, *right, *deps)
    return out[: len(parts)], out[len(parts) :]


def ring_z(pairs):
    r = pairs[0].shape[0] // 2
    chain, back = [pairs], []
    for _ in range(3):
        chain.append([send(p, ALONG_Z) for p in chain[-1]])
        back.append(send(jnp.concatenate(chain[-1]), OTHER))
    chain.append([send(p[:r], ALONG_Z) for p in chain[3]])
    back.append(send(jnp.concatenate(chain[-1]), OTHER))
    return chain, back


def on_device(
    ladder_amps, vvvv_slice, cd_live, amplitudes, hole_inter, direct, occ_energy, vir_energy
):
    z, core = lax.axis_index("vr"), lax.axis_index("vc")
    mine = jnp.concatenate([ladder_amps, hole_inter], axis=1)
    device = (lax.axis_index("occ") * NZ + z) * NC + core
    idx = lax.dynamic_slice_in_dim(jnp.asarray(places()), device, 1, 0)[0]
    n_first = sum(PARTS[:2])

    r = mine.shape[0]
    mine = send(mine, SLOTS)
    other = send(mine, OTHER)
    parts = [slice(s * r // STREAMS, (s + 1) * r // STREAMS) for s in range(STREAMS)]
    pairs = [jnp.concatenate([mine[p], other[p]]) for p in parts]
    chain, back = ring_z(pairs)
    xs = [x for c in chain for x in c] + back

    firsts = []
    for tiles in ROUNDS:
        (s1p, s1m), right = product(idx[:n_first], cd_live, xs, r, (vvvv_slice, amplitudes), PARTS[:2], tiles)
        firsts.append((right, send(s1p, first(1)), send(s1m, first(-1))))

    seconds, deps = [], ()
    for right, r1p, r1m in reversed(firsts):
        (mp, mm, own), _ = product(idx[n_first:], cd_live, xs, r, right, PARTS[2:], deps=deps)
        deps = (mm,)
        r2p, r2m = send(mp + r1p[: 2 * r], first(1)), send(mm + r1m[: 2 * r], first(-1))
        seconds.append((own[: 2 * r] + r2p + r1m[2 * r :], own[2 * r :] + r1p[2 * r :] + r2m))
    seconds.reverse()

    summed = []
    for g01, g23 in seconds:
        near, far, back = send(g01[r:], second(1)), send(g23[:r], second(2)), send(g23[r:], second(-1))
        summed.append(g01[:r] + near + far + back)
    summed = jnp.concatenate(summed, axis=1)
    return (direct + summed) / (vir_energy[None, :] - occ_energy[:, None])


def solution(mesh):
    in_specs = (
        P("occ", ("vr", "vc")),
        P("occ", ("vr", "vc")),
        P("occ"),
        P("occ", ("vr", "vc")),
        P("occ", ("vr", "vc")),
        P("occ", ("vr", "vc")),
        P("occ"),
        P(("vr", "vc")),
    )
    out_specs = P("occ", ("vr", "vc"))
    return jax.shard_map(
        on_device, mesh=mesh, in_specs=in_specs, out_specs=out_specs, check_vma=False
    )
```

time: 153 us -> 144 us (0.941)
  the two profiles are of different devices: /device:TPU:8 before, /device:TPU:150 now
where the time goes in v3:
time: 144 us
  waiting for transfers between devices  83 us (58%)
  Pallas kernels  33.9 us (24%)
  starting transfers between devices  22.6 us (16%)
  other arithmetic  3.29 us (2%)
    ppermute x28, waiting for transfers between devices, send(): return lax.ppermute(x, AXES, p)  83 us
    pallas_call x4, Pallas kernels, product(): pl.pallas_call(functools.partial(product_kernel, len(xs), len(deps), cd,...  33.9 us
    ppermute x28, starting transfers between devices, send(): return lax.ppermute(x, AXES, p)  22.6 us
  transfers between devices with their start and end apart: 28, of which 18 were waited for; matrix products, arithmetic and copies ran while one was open for 1% of the time, Pallas kernels for 17%

profile of v3, /device:TPU:150, one launch (start us, length us, event | category | flops | bytes accessed | tf_op | source)
XLA Modules:
  0.0 144.0 jit_solution(11692158792830558156)
XLA Ops:
  0.0 1.0 pad_maximum_fusion.3
  1.0 2.1 %collective-permute-start = (f32[64,832]{1,0:T(8,128)S(1)}, f32[64,832]{1,0:T(8,128)S(1)}, u32[]{:S(2)}, u32[]{:S(2)}) collective-permute-start(f32[64,832]{1,0:T(8,128)S(1)} %pad_maximum_fusion.3), channel_id=1, source_target_pairs={{0,3},{1,29},{2,47},{3,53},{4,79},{5,89},{6,103},{7,115},{8,135},{... | collective-permute-start | bytes 638984 | tf_op jit(solution)/shard_map/ppermute | solution.py:87
  3.0 8.9 %collective-permute-done = f32[64,832]{1,0:T(8,128)S(1)} collective-permute-done((f32[64,832]{1,0:T(8,128)S(1)}, f32[64,832]{1,0:T(8,128)S(1)}, u32[]{:S(2)}, u32[]{:S(2)}) %collective-permute-start) | collective-permute-done | bytes 213024 | tf_op jit(solution)/shard_map/ppermute | solution.py:87
  11.9 2.5 %collective-permute-start.1 = (f32[64,832]{1,0:T(8,128)S(1)}, f32[64,832]{1,0:T(8,128)S(1)}, u32[]{:S(2)}, u32[]{:S(2)}) collective-permute-start(f32[64,832]{1,0:T(8,128)S(1)} %collective-permute-done), channel_id=1, source_target_pairs={{0,1},{1,0},{2,3},{3,2},{4,5},{5,4},{6,7},{7,6},{8,9},{9,8},{10,11... | collective-permute-start | bytes 638984 | tf_op jit(solution)/shard_map/ppermute | solution.py:87
  14.5 1.1 collective-permute-done.1
  15.6 0.1 collective-permute-start.2
  15.8 10.8 %collective-permute-done.2 = f32[64,832]{1,0:T(8,128)S(1)} collective-permute-done((f32[64,832]{1,0:T(8,128)S(1)}, f32[64,832]{1,0:T(8,128)S(1)}, u32[]{:S(2)}, u32[]{:S(2)}) %collective-permute-start.2) | collective-permute-done | bytes 213024 | tf_op jit(solution)/shard_map/ppermute | solution.py:87
  26.6 2.5 %collective-permute-done.3 = f32[64,832]{1,0:T(8,128)S(1)} collective-permute-done((f32[64,832]{1,0:T(8,128)S(1)}, f32[64,832]{1,0:T(8,128)S(1)}, u32[]{:S(2)}, u32[]{:S(2)}) %collective-permute-start.3) | collective-permute-done | bytes 213024 | tf_op jit(solution)/shard_map/ppermute | solution.py:87
  29.1 4.8 %collective-permute-done.4 = f32[64,832]{1,0:T(8,128)S(1)} collective-permute-done((f32[64,832]{1,0:T(8,128)S(1)}, f32[64,832]{1,0:T(8,128)S(1)}, u32[]{:S(2)}, u32[]{:S(2)}) %collective-permute-start.4) | collective-permute-done | bytes 213024 | tf_op jit(solution)/shard_map/ppermute | solution.py:87
  33.9 2.5 %collective-permute-done.5 = f32[64,832]{1,0:T(8,128)S(1)} collective-permute-done((f32[64,832]{1,0:T(8,128)S(1)}, f32[64,832]{1,0:T(8,128)S(1)}, u32[]{:S(2)}, u32[]{:S(2)}) %collective-permute-start.5) | collective-permute-done | bytes 213024 | tf_op jit(solution)/shard_map/ppermute | solution.py:87
  36.4 0.9 collective-permute-start.10
  37.3 0.1 collective-permute-start.11
  37.4 3.7 %collective-permute-done.6 = f32[64,832]{1,0:T(8,128)S(1)} collective-permute-done((f32[64,832]{1,0:T(8,128)S(1)}, f32[64,832]{1,0:T(8,128)S(1)}, u32[]{:S(2)}, u32[]{:S(2)}) %collective-permute-start.6) | collective-permute-done | bytes 213024 | tf_op jit(solution)/shard_map/ppermute | solution.py:87
  41.2 2.4 %collective-permute-done.7 = f32[64,832]{1,0:T(8,128)S(1)} collective-permute-done((f32[64,832]{1,0:T(8,128)S(1)}, f32[64,832]{1,0:T(8,128)S(1)}, u32[]{:S(2)}, u32[]{:S(2)}) %collective-permute-start.7) | collective-permute-done | bytes 213024 | tf_op jit(solution)/shard_map/ppermute | solution.py:87
  43.7 0.1 collective-permute-start.12
  43.8 0.7 constant_dynamic-slice_fusion
  44.5 2.7 %collective-permute-done.8 = f32[32,832]{1,0:T(8,128)S(1)} collective-permute-done((f32[32,832]{1,0:T(8,128)S(1)}, f32[32,832]{1,0:T(8,128)S(1)}, u32[]{:S(2)}, u32[]{:S(2)}) %collective-permute-start.8) | collective-permute-done | bytes 106528 | tf_op jit(solution)/shard_map/ppermute | solution.py:87
  47.2 2.5 %collective-permute-done.9 = f32[32,832]{1,0:T(8,128)S(1)} collective-permute-done((f32[32,832]{1,0:T(8,128)S(1)}, f32[32,832]{1,0:T(8,128)S(1)}, u32[]{:S(2)}, u32[]{:S(2)}) %collective-permute-start.9) | collective-permute-done | bytes 106528 | tf_op jit(solution)/shard_map/ppermute | solution.py:87
  49.7 0.1 collective-permute-start.13
  49.8 1.4 collective-permute-done.13
  51.2 9.5 %product.5 = (f32[256,1408]{1,0:T(8,128)S(1)}, f32[256,1408]{1,0:T(8,128)S(1)}, bf16[768,1408]{1,0:T(8,128)(2,1)}, bf16[768,1408]{1,0:T(8,128)(2,1)}, bf16[192,1408]{1,0:T(8,128)(2,1)}) custom-call(s32[8]{0:T(128)S(1)} %get-tuple-element.49.idx_ref, s32[12]{0:T(128)S(1)} %copy-done, f32[2,32,832]{2,1,0:T(8,128)S(1)} %bitcast.38, f32[2,32,832]{2,1,0:T(8,128)S(1)} %bitcast.46, ...), custom_call_target="tpu_custom_call" | custom-call | flops 1000 | bytes 1000 | tf_op jit(solution)/shard_map/product/pallas_call | solution.py:167
  60.7 1.4 %collective-permute-start.21 = (f32[256,1408]{1,0:T(8,128)S(1)}, f32[256,1408]{1,0:T(8,128)S(1)}, u32[]{:S(2)}, u32[]{:S(2)}) collective-permute-start(f32[256,1408]{1,0:T(8,128)S(1)} %get-tuple-element.35), channel_id=1, source_target_pairs={{0,64},{1,17},{2,66},{3,19},{4,68},{5,21},{6,70},{7,23},{8,72},{9,... | collective-permute-start | bytes 4325384 | tf_op jit(solution)/shard_map/ppermute | solution.py:87
  62.2 0.6 collective-permute-start.23
  62.7 9.4 %product.4 = (f32[256,1536]{1,0:T(8,128)S(1)}, f32[256,1536]{1,0:T(8,128)S(1)}, bf16[768,1536]{1,0:T(8,128)(2,1)}, bf16[768,1536]{1,0:T(8,128)(2,1)}, bf16[192,1536]{1,0:T(8,128)(2,1)}) custom-call(s32[8]{0:T(128)S(1)} %get-tuple-element.49.idx_ref, s32[12]{0:T(128)S(1)} %copy-done, f32[2,32,832]{2,1,0:T(8,128)S(1)} %bitcast.39, f32[2,32,832]{2,1,0:T(8,128)S(1)} %bitcast.47, ...), custom_call_target="tpu_custom_call" | custom-call | flops 1000 | bytes 1000 | tf_op jit(solution)/shard_map/product/pallas_call | solution.py:167
  72.2 2.7 %collective-permute-start.14 = (f32[256,1536]{1,0:T(8,128)S(1)}, f32[256,1536]{1,0:T(8,128)S(1)}, u32[]{:S(2)}, u32[]{:S(2)}) collective-permute-start(f32[256,1536]{1,0:T(8,128)S(1)} %get-tuple-element.30), channel_id=1, source_target_pairs={{0,64},{1,17},{2,66},{3,19},{4,68},{5,21},{6,70},{7,23},{8,72},{9,... | collective-permute-start | bytes 4718600 | tf_op jit(solution)/shard_map/ppermute | solution.py:87
  74.8 7.6 %product.6 = (f32[128,1408]{1,0:T(8,128)S(1)}, f32[128,1408]{1,0:T(8,128)S(1)}, f32[256,1408]{1,0:T(8,128)S(1)}) custom-call(s32[8]{0:T(128)S(1)} %get-tuple-element.50.idx_ref, s32[12]{0:T(128)S(1)} %copy-done, f32[2,32,832]{2,1,0:T(8,128)S(1)} %bitcast.40, f32[2,32,832]{2,1,0:T(8,128)S(1)} %bitcast.48, f32[2,32,832]{2,1,0:T(8,128)S(1)} %bitcast.44, ...), custom_call_target="tpu_custom_call" | custom-call | flops 1000 | bytes 1000 | tf_op jit(solution)/shard_map/product/pallas_call | solution.py:167
  82.5 7.4 %product.7 = (f32[128,1536]{1,0:T(8,128)S(1)}, f32[128,1536]{1,0:T(8,128)S(1)}, f32[256,1536]{1,0:T(8,128)S(1)}) custom-call(s32[8]{0:T(128)S(1)} %get-tuple-element.50.idx_ref, s32[12]{0:T(128)S(1)} %copy-done, f32[2,32,832]{2,1,0:T(8,128)S(1)} %bitcast.41, f32[2,32,832]{2,1,0:T(8,128)S(1)} %bitcast.49, f32[2,32,832]{2,1,0:T(8,128)S(1)} %bitcast.45, ...), custom_call_target="tpu_custom_call" | custom-call | flops 1000 | bytes 1000 | tf_op jit(solution)/shard_map/product/pallas_call | solution.py:167
  89.9 3.3 %collective-permute-start.22 = (f32[128,1408]{1,0:T(8,128)S(1)}, f32[128,1408]{1,0:T(8,128)S(1)}, u32[]{:S(2)}, u32[]{:S(2)}) collective-permute-start(f32[128,1408]{1,0:T(8,128)S(1)} %slice_add_fusion.7), channel_id=1, source_target_pairs={{0,64},{1,17},{2,66},{3,19},{4,68},{5,21},{6,70},{7,23},{8,72},{9,... | collective-permute-start | bytes 2162696 | tf_op jit(solution)/shard_map/ppermute | solution.py:87
  93.2 0.1 slice_add_fusion.4
  93.4 3.2 %collective-permute-done.14 = f32[256,1536]{1,0:T(8,128)S(1)} collective-permute-done((f32[256,1536]{1,0:T(8,128)S(1)}, f32[256,1536]{1,0:T(8,128)S(1)}, u32[]{:S(2)}, u32[]{:S(2)}) %collective-permute-start.14) | collective-permute-done | bytes 1572896 | tf_op jit(solution)/shard_map/ppermute | solution.py:87
  96.6 0.1 slice_add_fusion.3
  96.7 2.7 %collective-permute-start.15 = (f32[128,1536]{1,0:T(8,128)S(1)}, f32[128,1536]{1,0:T(8,128)S(1)}, u32[]{:S(2)}, u32[]{:S(2)}) collective-permute-start(f32[128,1536]{1,0:T(8,128)S(1)} %slice_add_fusion.3), channel_id=1, source_target_pairs={{0,64},{1,17},{2,66},{3,19},{4,68},{5,21},{6,70},{7,23},{8,72},{9,... | collective-permute-start | bytes 2359304 | tf_op jit(solution)/shard_map/ppermute | solution.py:87
  99.4 0.1 slice_add_fusion
  99.6 4.7 %collective-permute-done.22 = f32[128,1408]{1,0:T(8,128)S(1)} collective-permute-done((f32[128,1408]{1,0:T(8,128)S(1)}, f32[128,1408]{1,0:T(8,128)S(1)}, u32[]{:S(2)}, u32[]{:S(2)}) %collective-permute-start.22) | collective-permute-done | bytes 720928 | tf_op jit(solution)/shard_map/ppermute | solution.py:87
  104.3 2.7 %collective-permute-done.25 = f32[128,1408]{1,0:T(8,128)S(1)} collective-permute-done((f32[128,1408]{1,0:T(8,128)S(1)}, f32[128,1408]{1,0:T(8,128)S(1)}, u32[]{:S(2)}, u32[]{:S(2)}) %collective-permute-start.25) | collective-permute-done | bytes 720928 | tf_op jit(solution)/shard_map/ppermute | solution.py:87
  107.0 0.2 slice_add_fusion.6
  107.2 1.7 %collective-permute-start.24 = (f32[64,1408]{1,0:T(8,128)S(1)}, f32[64,1408]{1,0:T(8,128)S(1)}, u32[]{:S(2)}, u32[]{:S(2)}) collective-permute-start(f32[64,1408]{1,0:T(8,128)S(1)} %slice.139), channel_id=1, source_target_pairs={{0,16},{1,65},{2,18},{3,67},{4,20},{5,69},{6,22},{7,71},{8,24},{9,... | collective-permute-start | bytes 1081352 | tf_op jit(solution)/shard_map/ppermute | solution.py:87
  109.0 0.1 collective-permute-start.26
  109.1 1.5 %collective-permute-start.27 = (f32[64,1408]{1,0:T(8,128)S(1)}, f32[64,1408]{1,0:T(8,128)S(1)}, u32[]{:S(2)}, u32[]{:S(2)}) collective-permute-start(f32[64,1408]{1,0:T(8,128)S(1)} %get-tuple-element.44), channel_id=1, source_target_pairs={{0,48},{1,193},{2,50},{3,195},{4,52},{5,197},{6,54},{7,199},{8,56}... | collective-permute-start | bytes 1081352 | tf_op jit(solution)/shard_map/ppermute | solution.py:87
  110.5 8.2 %collective-permute-done.15 = f32[128,1536]{1,0:T(8,128)S(1)} collective-permute-done((f32[128,1536]{1,0:T(8,128)S(1)}, f32[128,1536]{1,0:T(8,128)S(1)}, u32[]{:S(2)}, u32[]{:S(2)}) %collective-permute-start.15) | collective-permute-done | bytes 786464 | tf_op jit(solution)/shard_map/ppermute | solution.py:87
  118.7 9.4 %collective-permute-done.18 = f32[128,1536]{1,0:T(8,128)S(1)} collective-permute-done((f32[128,1536]{1,0:T(8,128)S(1)}, f32[128,1536]{1,0:T(8,128)S(1)}, u32[]{:S(2)}, u32[]{:S(2)}) %collective-permute-start.18) | collective-permute-done | bytes 786464 | tf_op jit(solution)/shard_map/ppermute | solution.py:87
  128.1 0.4 slice_add_fusion.2
  128.7 1.4 collective-permute-start.19
  130.1 0.8 collective-permute-start.20
  131.0 9.6 %collective-permute-done.17 = f32[64,1536]{1,0:T(8,128)S(1)} collective-permute-done((f32[64,1536]{1,0:T(8,128)S(1)}, f32[64,1536]{1,0:T(8,128)S(1)}, u32[]{:S(2)}, u32[]{:S(2)}) %collective-permute-start.17) | collective-permute-done | bytes 393248 | tf_op jit(solution)/shard_map/ppermute | solution.py:87
  140.6 2.3 %collective-permute-done.20 = f32[64,1536]{1,0:T(8,128)S(1)} collective-permute-done((f32[64,1536]{1,0:T(8,128)S(1)}, f32[64,1536]{1,0:T(8,128)S(1)}, u32[]{:S(2)}, u32[]{:S(2)}) %collective-permute-start.20) | collective-permute-done | bytes 393248 | tf_op jit(solution)/shard_map/ppermute | solution.py:87
  142.8 0.1 fusion.4
  143.0 1.0 fusion.1
  (46 shorter events, 1.1 us)
Async XLA Ops:
  1.0 11.0 %collective-permute-start = (f32[64,832]{1,0:T(8,128)S(1)}, f32[64,832]{1,0:T(8,128)S(1)}, u32[]{:S(2)}, u32[]{:S(2)}) collective-permute-start(f32[64,832]{1,0:T(8,128)S(1)} %pad_maximum_fusion.3), channel_id=1, source_target_pairs={{0,3},{1,29},{2,47},{3,53},{4,79},{5,89},{6,103},{7,115},{8,135},{... | collective-permute-start | bytes 638984 | tf_op jit(solution)/shard_map/ppermute | solution.py:87
  11.9 3.6 %collective-permute-start.1 = (f32[64,832]{1,0:T(8,128)S(1)}, f32[64,832]{1,0:T(8,128)S(1)}, u32[]{:S(2)}, u32[]{:S(2)}) collective-permute-start(f32[64,832]{1,0:T(8,128)S(1)} %collective-permute-done), channel_id=1, source_target_pairs={{0,1},{1,0},{2,3},{3,2},{4,5},{5,4},{6,7},{7,6},{8,9},{9,8},{10,11... | collective-permute-start | bytes 638984 | tf_op jit(solution)/shard_map/ppermute | solution.py:87
  15.6 11.0 %collective-permute-start.2 = (f32[64,832]{1,0:T(8,128)S(1)}, f32[64,832]{1,0:T(8,128)S(1)}, u32[]{:S(2)}, u32[]{:S(2)}) collective-permute-start(f32[64,832]{1,0:T(8,128)S(1)} %pad_maximum_fusion.4), channel_id=1, source_target_pairs={{0,2},{1,15},{2,4},{3,1},{4,6},{5,3},{6,8},{7,5},{8,10},{9,7},{10,... | collective-permute-start | bytes 638984 | tf_op jit(solution)/shard_map/ppermute | solution.py:87
  15.7 13.3 %collective-permute-start.3 = (f32[64,832]{1,0:T(8,128)S(1)}, f32[64,832]{1,0:T(8,128)S(1)}, u32[]{:S(2)}, u32[]{:S(2)}) collective-permute-start(f32[64,832]{1,0:T(8,128)S(1)} %pad_maximum_fusion.5), channel_id=1, source_target_pairs={{0,2},{1,15},{2,4},{3,1},{4,6},{5,3},{6,8},{7,5},{8,10},{9,7},{10,... | collective-permute-start | bytes 638984 | tf_op jit(solution)/shard_map/ppermute | solution.py:87
  26.6 7.2 %collective-permute-start.4 = (f32[64,832]{1,0:T(8,128)S(1)}, f32[64,832]{1,0:T(8,128)S(1)}, u32[]{:S(2)}, u32[]{:S(2)}) collective-permute-start(f32[64,832]{1,0:T(8,128)S(1)} %collective-permute-done.2), channel_id=1, source_target_pairs={{0,2},{1,15},{2,4},{3,1},{4,6},{5,3},{6,8},{7,5},{8,10},{9,7},{10,... | collective-permute-start | bytes 638984 | tf_op jit(solution)/shard_map/ppermute | solution.py:87
  29.1 7.2 %collective-permute-start.5 = (f32[64,832]{1,0:T(8,128)S(1)}, f32[64,832]{1,0:T(8,128)S(1)}, u32[]{:S(2)}, u32[]{:S(2)}) collective-permute-start(f32[64,832]{1,0:T(8,128)S(1)} %collective-permute-done.3), channel_id=1, source_target_pairs={{0,2},{1,15},{2,4},{3,1},{4,6},{5,3},{6,8},{7,5},{8,10},{9,7},{10,... | collective-permute-start | bytes 638984 | tf_op jit(solution)/shard_map/ppermute | solution.py:87
  33.8 7.2 %collective-permute-start.6 = (f32[64,832]{1,0:T(8,128)S(1)}, f32[64,832]{1,0:T(8,128)S(1)}, u32[]{:S(2)}, u32[]{:S(2)}) collective-permute-start(f32[64,832]{1,0:T(8,128)S(1)} %collective-permute-done.4), channel_id=1, source_target_pairs={{0,2},{1,15},{2,4},{3,1},{4,6},{5,3},{6,8},{7,5},{8,10},{9,7},{10,... | collective-permute-start | bytes 638984 | tf_op jit(solution)/shard_map/ppermute | solution.py:87
  36.3 7.2 %collective-permute-start.7 = (f32[64,832]{1,0:T(8,128)S(1)}, f32[64,832]{1,0:T(8,128)S(1)}, u32[]{:S(2)}, u32[]{:S(2)}) collective-permute-start(f32[64,832]{1,0:T(8,128)S(1)} %collective-permute-done.5), channel_id=1, source_target_pairs={{0,2},{1,15},{2,4},{3,1},{4,6},{5,3},{6,8},{7,5},{8,10},{9,7},{10,... | collective-permute-start | bytes 638984 | tf_op jit(solution)/shard_map/ppermute | solution.py:87
  36.3 14.9 %copy-start = (s32[12]{0:T(128)S(1)}, s32[12]{0:T(128)}, u32[]{:S(2)}) copy-start(s32[12]{0:T(128)} %live_ref.7) | copy-start | bytes 148
  36.4 13.5 %collective-permute-start.10 = (f32[128,832]{1,0:T(8,128)S(1)}, f32[128,832]{1,0:T(8,128)S(1)}, u32[]{:S(2)}, u32[]{:S(2)}) collective-permute-start(f32[128,832]{1,0:T(8,128)S(1)} %pad_maximum_fusion), channel_id=1, source_target_pairs={{0,1},{1,0},{2,3},{3,2},{4,5},{5,4},{6,7},{7,6},{8,9},{9,8},{10,11... | collective-permute-start | bytes 1277960 | tf_op jit(solution)/shard_map/ppermute | solution.py:87
  37.3 12.6 %collective-permute-start.11 = (f32[128,832]{1,0:T(8,128)S(1)}, f32[128,832]{1,0:T(8,128)S(1)}, u32[]{:S(2)}, u32[]{:S(2)}) collective-permute-start(f32[128,832]{1,0:T(8,128)S(1)} %pad_maximum_fusion.1), channel_id=1, source_target_pairs={{0,1},{1,0},{2,3},{3,2},{4,5},{5,4},{6,7},{7,6},{8,9},{9,8},{10,11... | collective-permute-start | bytes 1277960 | tf_op jit(solution)/shard_map/ppermute | solution.py:87
  41.1 6.1 %collective-permute-start.8 = (f32[32,832]{1,0:T(8,128)S(1)}, f32[32,832]{1,0:T(8,128)S(1)}, u32[]{:S(2)}, u32[]{:S(2)}) collective-permute-start(f32[32,832]{1,0:T(8,128)S(1)} %slice.126), channel_id=1, source_target_pairs={{0,2},{1,15},{2,4},{3,1},{4,6},{5,3},{6,8},{7,5},{8,10},{9,7},{10,... | collective-permute-start | bytes 319496 | tf_op jit(solution)/shard_map/ppermute | solution.py:87
  43.6 6.1 %collective-permute-start.9 = (f32[32,832]{1,0:T(8,128)S(1)}, f32[32,832]{1,0:T(8,128)S(1)}, u32[]{:S(2)}, u32[]{:S(2)}) collective-permute-start(f32[32,832]{1,0:T(8,128)S(1)} %slice.127), channel_id=1, source_target_pairs={{0,2},{1,15},{2,4},{3,1},{4,6},{5,3},{6,8},{7,5},{8,10},{9,7},{10,... | collective-permute-start | bytes 319496 | tf_op jit(solution)/shard_map/ppermute | solution.py:87
  43.7 7.5 %collective-permute-start.12 = (f32[128,832]{1,0:T(8,128)S(1)}, f32[128,832]{1,0:T(8,128)S(1)}, u32[]{:S(2)}, u32[]{:S(2)}) collective-permute-start(f32[128,832]{1,0:T(8,128)S(1)} %pad_maximum_fusion.2), channel_id=1, source_target_pairs={{0,1},{1,0},{2,3},{3,2},{4,5},{5,4},{6,7},{7,6},{8,9},{9,8},{10,11... | collective-permute-start | bytes 1277960 | tf_op jit(solution)/shard_map/ppermute | solution.py:87
  49.7 1.6 %collective-permute-start.13 = (f32[64,832]{1,0:T(8,128)S(1)}, f32[64,832]{1,0:T(8,128)S(1)}, u32[]{:S(2)}, u32[]{:S(2)}) collective-permute-start(f32[64,832]{1,0:T(8,128)S(1)} %pad_maximum_fusion.6), channel_id=1, source_target_pairs={{0,1},{1,0},{2,3},{3,2},{4,5},{5,4},{6,7},{7,6},{8,9},{9,8},{10,11... | collective-permute-start | bytes 638984 | tf_op jit(solution)/shard_map/ppermute | solution.py:87
  60.7 29.1 %collective-permute-start.21 = (f32[256,1408]{1,0:T(8,128)S(1)}, f32[256,1408]{1,0:T(8,128)S(1)}, u32[]{:S(2)}, u32[]{:S(2)}) collective-permute-start(f32[256,1408]{1,0:T(8,128)S(1)} %get-tuple-element.35), channel_id=1, source_target_pairs={{0,64},{1,17},{2,66},{3,19},{4,68},{5,21},{6,70},{7,23},{8,72},{9,... | collective-permute-start | bytes 4325384 | tf_op jit(solution)/shard_map/ppermute | solution.py:87
  62.2 31.1 %collective-permute-start.23 = (f32[256,1408]{1,0:T(8,128)S(1)}, f32[256,1408]{1,0:T(8,128)S(1)}, u32[]{:S(2)}, u32[]{:S(2)}) collective-permute-start(f32[256,1408]{1,0:T(8,128)S(1)} %get-tuple-element.36), channel_id=1, source_target_pairs={{0,192},{1,49},{2,194},{3,51},{4,196},{5,53},{6,198},{7,55},{8,200... | collective-permute-start | bytes 4325384 | tf_op jit(solution)/shard_map/ppermute | solution.py:87
  72.2 24.4 %collective-permute-start.14 = (f32[256,1536]{1,0:T(8,128)S(1)}, f32[256,1536]{1,0:T(8,128)S(1)}, u32[]{:S(2)}, u32[]{:S(2)}) collective-permute-start(f32[256,1536]{1,0:T(8,128)S(1)} %get-tuple-element.30), channel_id=1, source_target_pairs={{0,64},{1,17},{2,66},{3,19},{4,68},{5,21},{6,70},{7,23},{8,72},{9,... | collective-permute-start | bytes 4718600 | tf_op jit(solution)/shard_map/ppermute | solution.py:87
  74.8 24.6 %collective-permute-start.16 = (f32[256,1536]{1,0:T(8,128)S(1)}, f32[256,1536]{1,0:T(8,128)S(1)}, u32[]{:S(2)}, u32[]{:S(2)}) collective-permute-start(f32[256,1536]{1,0:T(8,128)S(1)} %get-tuple-element.31), channel_id=1, source_target_pairs={{0,192},{1,49},{2,194},{3,51},{4,196},{5,53},{6,198},{7,55},{8,200... | collective-permute-start | bytes 4718600 | tf_op jit(solution)/shard_map/ppermute | solution.py:87
  89.9 14.4 %collective-permute-start.22 = (f32[128,1408]{1,0:T(8,128)S(1)}, f32[128,1408]{1,0:T(8,128)S(1)}, u32[]{:S(2)}, u32[]{:S(2)}) collective-permute-start(f32[128,1408]{1,0:T(8,128)S(1)} %slice_add_fusion.7), channel_id=1, source_target_pairs={{0,64},{1,17},{2,66},{3,19},{4,68},{5,21},{6,70},{7,23},{8,72},{9,... | collective-permute-start | bytes 2162696 | tf_op jit(solution)/shard_map/ppermute | solution.py:87
  93.3 13.6 %collective-permute-start.25 = (f32[128,1408]{1,0:T(8,128)S(1)}, f32[128,1408]{1,0:T(8,128)S(1)}, u32[]{:S(2)}, u32[]{:S(2)}) collective-permute-start(f32[128,1408]{1,0:T(8,128)S(1)} %slice_add_fusion.4), channel_id=1, source_target_pairs={{0,192},{1,49},{2,194},{3,51},{4,196},{5,53},{6,198},{7,55},{8,200... | collective-permute-start | bytes 2162696 | tf_op jit(solution)/shard_map/ppermute | solution.py:87
  96.7 22.0 %collective-permute-start.15 = (f32[128,1536]{1,0:T(8,128)S(1)}, f32[128,1536]{1,0:T(8,128)S(1)}, u32[]{:S(2)}, u32[]{:S(2)}) collective-permute-start(f32[128,1536]{1,0:T(8,128)S(1)} %slice_add_fusion.3), channel_id=1, source_target_pairs={{0,64},{1,17},{2,66},{3,19},{4,68},{5,21},{6,70},{7,23},{8,72},{9,... | collective-permute-start | bytes 2359304 | tf_op jit(solution)/shard_map/ppermute | solution.py:87
  99.5 28.6 %collective-permute-start.18 = (f32[128,1536]{1,0:T(8,128)S(1)}, f32[128,1536]{1,0:T(8,128)S(1)}, u32[]{:S(2)}, u32[]{:S(2)}) collective-permute-start(f32[128,1536]{1,0:T(8,128)S(1)} %slice_add_fusion), channel_id=1, source_target_pairs={{0,192},{1,49},{2,194},{3,51},{4,196},{5,53},{6,198},{7,55},{8,200... | collective-permute-start | bytes 2359304 | tf_op jit(solution)/shard_map/ppermute | solution.py:87
  107.2 22.9 %collective-permute-start.24 = (f32[64,1408]{1,0:T(8,128)S(1)}, f32[64,1408]{1,0:T(8,128)S(1)}, u32[]{:S(2)}, u32[]{:S(2)}) collective-permute-start(f32[64,1408]{1,0:T(8,128)S(1)} %slice.139), channel_id=1, source_target_pairs={{0,16},{1,65},{2,18},{3,67},{4,20},{5,69},{6,22},{7,71},{8,24},{9,... | collective-permute-start | bytes 1081352 | tf_op jit(solution)/shard_map/ppermute | solution.py:87
  109.0 21.9 %collective-permute-start.26 = (f32[64,1408]{1,0:T(8,128)S(1)}, f32[64,1408]{1,0:T(8,128)S(1)}, u32[]{:S(2)}, u32[]{:S(2)}) collective-permute-start(f32[64,1408]{1,0:T(8,128)S(1)} %get-tuple-element.43), channel_id=1, source_target_pairs={{0,32},{1,129},{2,34},{3,131},{4,36},{5,133},{6,38},{7,135},{8,40}... | collective-permute-start | bytes 1081352 | tf_op jit(solution)/shard_map/ppermute | solution.py:87
  109.1 21.8 %collective-permute-start.27 = (f32[64,1408]{1,0:T(8,128)S(1)}, f32[64,1408]{1,0:T(8,128)S(1)}, u32[]{:S(2)}, u32[]{:S(2)}) collective-permute-start(f32[64,1408]{1,0:T(8,128)S(1)} %get-tuple-element.44), channel_id=1, source_target_pairs={{0,48},{1,193},{2,50},{3,195},{4,52},{5,197},{6,54},{7,199},{8,56}... | collective-permute-start | bytes 1081352 | tf_op jit(solution)/shard_map/ppermute | solution.py:87
  128.5 12.1 %collective-permute-start.17 = (f32[64,1536]{1,0:T(8,128)S(1)}, f32[64,1536]{1,0:T(8,128)S(1)}, u32[]{:S(2)}, u32[]{:S(2)}) collective-permute-start(f32[64,1536]{1,0:T(8,128)S(1)} %slice.131), channel_id=1, source_target_pairs={{0,16},{1,65},{2,18},{3,67},{4,20},{5,69},{6,22},{7,71},{8,24},{9,... | collective-permute-start | bytes 1179656 | tf_op jit(solution)/shard_map/ppermute | solution.py:87
  128.7 11.9 %collective-permute-start.19 = (f32[64,1536]{1,0:T(8,128)S(1)}, f32[64,1536]{1,0:T(8,128)S(1)}, u32[]{:S(2)}, u32[]{:S(2)}) collective-permute-start(f32[64,1536]{1,0:T(8,128)S(1)} %get-tuple-element.41), channel_id=1, source_target_pairs={{0,32},{1,129},{2,34},{3,131},{4,36},{5,133},{6,38},{7,135},{8,40}... | collective-permute-start | bytes 1179656 | tf_op jit(solution)/shard_map/ppermute | solution.py:87
  130.1 12.9 %copy-start.1 = (f32[64,2944]{1,0:T(8,128)S(1)}, f32[64,2944]{1,0:T(8,128)}, u32[]{:S(2)}) copy-start(f32[64,2944]{1,0:T(8,128)} %param.14) | copy-start | bytes 2260996
  130.1 12.9 %copy-start.2 = (f32[2944]{0:T(1024)S(1)}, f32[2944]{0:T(1024)}, u32[]{:S(2)}) copy-start(f32[2944]{0:T(1024)} %param.16) | copy-start | bytes 35332
  130.1 12.9 %copy-start.3 = (f32[64]{0:T(128)S(1)}, f32[64]{0:T(128)}, u32[]{:S(2)}) copy-start(f32[64]{0:T(128)} %param.15) | copy-start | bytes 772
  130.1 12.7 %collective-permute-start.20 = (f32[64,1536]{1,0:T(8,128)S(1)}, f32[64,1536]{1,0:T(8,128)S(1)}, u32[]{:S(2)}, u32[]{:S(2)}) collective-permute-start(f32[64,1536]{1,0:T(8,128)S(1)} %get-tuple-element.42), channel_id=1, source_target_pairs={{0,48},{1,193},{2,50},{3,195},{4,52},{5,197},{6,54},{7,199},{8,56}... | collective-permute-start | bytes 1179656 | tf_op jit(solution)/shard_map/ppermute | solution.py:87

commit v4 on v3

--- a/solution.py
+++ b/solution.py
@@ -231,11 +231,9 @@
         seconds.append((own[: 2 * r] + r2p + r1m[2 * r :], own[2 * r :] + r1p[2 * r :] + r2m))
     seconds.reverse()
 
-    summed = []
-    for g01, g23 in seconds:
-        near, far, back = send(g01[r:], second(1)), send(g23[:r], second(2)), send(g23[r:], second(-1))
-        summed.append(g01[:r] + near + far + back)
-    summed = jnp.concatenate(summed, axis=1)
+    g01, g23 = (jnp.concatenate(g, axis=1) for g in zip(*seconds))
+    near, far, back = send(g01[r:], second(1)), send(g23[:r], second(2)), send(g23[r:], second(-1))
+    summed = g01[:r] + near + far + back
     return (direct + summed) / (vir_energy[None, :] - occ_energy[:, None])
 
 

time: 144 us -> 141 us (0.979)
  the two profiles are of different devices: /device:TPU:150 before, /device:TPU:8 now
where the time goes in v4:
time: 141 us
  waiting for transfers between devices  66.2 us (47%)
  starting transfers between devices  36.9 us (26%)
  Pallas kernels  33.8 us (24%)
  other arithmetic  3.32 us (2%)
    ppermute x25, waiting for transfers between devices, send(): return lax.ppermute(x, AXES, p)  66.2 us
    ppermute x25, starting transfers between devices, send(): return lax.ppermute(x, AXES, p)  36.9 us
    pallas_call x4, Pallas kernels, product(): pl.pallas_call(functools.partial(product_kernel, len(xs), len(deps), cd,...  33.8 us
  transfers between devices with their start and end apart: 25, of which 16 were waited for; matrix products, arithmetic and copies ran while one was open for 1% of the time, Pallas kernels for 17%

profile of v4, /device:TPU:8, one launch (start us, length us, event | category | flops | bytes accessed | tf_op | source)
XLA Modules:
  0.0 141.2 jit_solution(11776785345460992764)
XLA Ops:
  0.0 1.0 pad_maximum_fusion.5
  1.0 7.1 %collective-permute-start = (f32[64,832]{1,0:T(8,128)S(1)}, f32[64,832]{1,0:T(8,128)S(1)}, u32[]{:S(2)}, u32[]{:S(2)}) collective-permute-start(f32[64,832]{1,0:T(8,128)S(1)} %pad_maximum_fusion.5), channel_id=1, source_target_pairs={{0,3},{1,29},{2,47},{3,53},{4,79},{5,89},{6,103},{7,115},{8,135},{... | collective-permute-start | bytes 638984 | tf_op jit(solution)/shard_map/ppermute | solution.py:87
  8.1 3.5 %collective-permute-done = f32[64,832]{1,0:T(8,128)S(1)} collective-permute-done((f32[64,832]{1,0:T(8,128)S(1)}, f32[64,832]{1,0:T(8,128)S(1)}, u32[]{:S(2)}, u32[]{:S(2)}) %collective-permute-start) | collective-permute-done | bytes 213024 | tf_op jit(solution)/shard_map/ppermute | solution.py:87
  11.6 3.4 %collective-permute-start.1 = (f32[64,832]{1,0:T(8,128)S(1)}, f32[64,832]{1,0:T(8,128)S(1)}, u32[]{:S(2)}, u32[]{:S(2)}) collective-permute-start(f32[64,832]{1,0:T(8,128)S(1)} %collective-permute-done), channel_id=1, source_target_pairs={{0,1},{1,0},{2,3},{3,2},{4,5},{5,4},{6,7},{7,6},{8,9},{9,8},{10,11... | collective-permute-start | bytes 638984 | tf_op jit(solution)/shard_map/ppermute | solution.py:87
  15.0 1.1 collective-permute-done.1
  16.2 3.0 %collective-permute-start.2 = (f32[64,832]{1,0:T(8,128)S(1)}, f32[64,832]{1,0:T(8,128)S(1)}, u32[]{:S(2)}, u32[]{:S(2)}) collective-permute-start(f32[64,832]{1,0:T(8,128)S(1)} %pad_maximum_fusion.6), channel_id=1, source_target_pairs={{0,2},{1,15},{2,4},{3,1},{4,6},{5,3},{6,8},{7,5},{8,10},{9,7},{10,... | collective-permute-start | bytes 638984 | tf_op jit(solution)/shard_map/ppermute | solution.py:87
  19.2 0.1 collective-permute-start.3
  19.3 6.2 %collective-permute-done.2 = f32[64,832]{1,0:T(8,128)S(1)} collective-permute-done((f32[64,832]{1,0:T(8,128)S(1)}, f32[64,832]{1,0:T(8,128)S(1)}, u32[]{:S(2)}, u32[]{:S(2)}) %collective-permute-start.2) | collective-permute-done | bytes 213024 | tf_op jit(solution)/shard_map/ppermute | solution.py:87
  25.5 2.5 %collective-permute-done.3 = f32[64,832]{1,0:T(8,128)S(1)} collective-permute-done((f32[64,832]{1,0:T(8,128)S(1)}, f32[64,832]{1,0:T(8,128)S(1)}, u32[]{:S(2)}, u32[]{:S(2)}) %collective-permute-start.3) | collective-permute-done | bytes 213024 | tf_op jit(solution)/shard_map/ppermute | solution.py:87
  28.0 1.0 collective-permute-start.5
  29.0 5.8 %collective-permute-done.4 = f32[64,832]{1,0:T(8,128)S(1)} collective-permute-done((f32[64,832]{1,0:T(8,128)S(1)}, f32[64,832]{1,0:T(8,128)S(1)}, u32[]{:S(2)}, u32[]{:S(2)}) %collective-permute-start.4) | collective-permute-done | bytes 213024 | tf_op jit(solution)/shard_map/ppermute | solution.py:87
  34.8 2.5 %collective-permute-done.5 = f32[64,832]{1,0:T(8,128)S(1)} collective-permute-done((f32[64,832]{1,0:T(8,128)S(1)}, f32[64,832]{1,0:T(8,128)S(1)}, u32[]{:S(2)}, u32[]{:S(2)}) %collective-permute-start.5) | collective-permute-done | bytes 213024 | tf_op jit(solution)/shard_map/ppermute | solution.py:87
  37.3 1.5 %collective-permute-start.10 = (f32[128,832]{1,0:T(8,128)S(1)}, f32[128,832]{1,0:T(8,128)S(1)}, u32[]{:S(2)}, u32[]{:S(2)}) collective-permute-start(f32[128,832]{1,0:T(8,128)S(1)} %pad_maximum_fusion.2), channel_id=1, source_target_pairs={{0,1},{1,0},{2,3},{3,2},{4,5},{5,4},{6,7},{7,6},{8,9},{9,8},{10,11... | collective-permute-start | bytes 1277960 | tf_op jit(solution)/shard_map/ppermute | solution.py:87
  38.8 0.1 collective-permute-start.11
  38.9 3.1 %collective-permute-done.6 = f32[64,832]{1,0:T(8,128)S(1)} collective-permute-done((f32[64,832]{1,0:T(8,128)S(1)}, f32[64,832]{1,0:T(8,128)S(1)}, u32[]{:S(2)}, u32[]{:S(2)}) %collective-permute-start.6) | collective-permute-done | bytes 213024 | tf_op jit(solution)/shard_map/ppermute | solution.py:87
  42.1 0.1 collective-permute-start.8
  42.2 2.4 %collective-permute-done.7 = f32[64,832]{1,0:T(8,128)S(1)} collective-permute-done((f32[64,832]{1,0:T(8,128)S(1)}, f32[64,832]{1,0:T(8,128)S(1)}, u32[]{:S(2)}, u32[]{:S(2)}) %collective-permute-start.7) | collective-permute-done | bytes 213024 | tf_op jit(solution)/shard_map/ppermute | solution.py:87
  44.5 0.1 collective-permute-start.9
  44.7 0.3 collective-permute-start.12
  45.0 0.7 constant_dynamic-slice_fusion
  45.7 2.5 %collective-permute-done.8 = f32[32,832]{1,0:T(8,128)S(1)} collective-permute-done((f32[32,832]{1,0:T(8,128)S(1)}, f32[32,832]{1,0:T(8,128)S(1)}, u32[]{:S(2)}, u32[]{:S(2)}) %collective-permute-start.8) | collective-permute-done | bytes 106528 | tf_op jit(solution)/shard_map/ppermute | solution.py:87
  48.2 2.5 %collective-permute-done.9 = f32[32,832]{1,0:T(8,128)S(1)} collective-permute-done((f32[32,832]{1,0:T(8,128)S(1)}, f32[32,832]{1,0:T(8,128)S(1)}, u32[]{:S(2)}, u32[]{:S(2)}) %collective-permute-start.9) | collective-permute-done | bytes 106528 | tf_op jit(solution)/shard_map/ppermute | solution.py:87
  50.6 0.1 collective-permute-start.13
  50.8 1.4 collective-permute-done.13
  52.2 9.5 %product.5 = (f32[256,1408]{1,0:T(8,128)S(1)}, f32[256,1408]{1,0:T(8,128)S(1)}, bf16[768,1408]{1,0:T(8,128)(2,1)}, bf16[768,1408]{1,0:T(8,128)(2,1)}, bf16[192,1408]{1,0:T(8,128)(2,1)}) custom-call(s32[8]{0:T(128)S(1)} %get-tuple-element.47.idx_ref, s32[12]{0:T(128)S(1)} %copy-done, f32[2,32,832]{2,1,0:T(8,128)S(1)} %bitcast.38, f32[2,32,832]{2,1,0:T(8,128)S(1)} %bitcast.46, ...), custom_call_target="tpu_custom_call" | custom-call | flops 1000 | bytes 1000 | tf_op jit(solution)/shard_map/product/pallas_call | solution.py:167
  61.7 1.1 collective-permute-start.17
  62.8 2.2 %collective-permute-start.19 = (f32[256,1408]{1,0:T(8,128)S(1)}, f32[256,1408]{1,0:T(8,128)S(1)}, u32[]{:S(2)}, u32[]{:S(2)}) collective-permute-start(f32[256,1408]{1,0:T(8,128)S(1)} %get-tuple-element.35), channel_id=1, source_target_pairs={{0,192},{1,49},{2,194},{3,51},{4,196},{5,53},{6,198},{7,55},{8,200... | collective-permute-start | bytes 4325384 | tf_op jit(solution)/shard_map/ppermute | solution.py:87
  64.9 9.4 %product.4 = (f32[256,1536]{1,0:T(8,128)S(1)}, f32[256,1536]{1,0:T(8,128)S(1)}, bf16[768,1536]{1,0:T(8,128)(2,1)}, bf16[768,1536]{1,0:T(8,128)(2,1)}, bf16[192,1536]{1,0:T(8,128)(2,1)}) custom-call(s32[8]{0:T(128)S(1)} %get-tuple-element.47.idx_ref, s32[12]{0:T(128)S(1)} %copy-done, f32[2,32,832]{2,1,0:T(8,128)S(1)} %bitcast.39, f32[2,32,832]{2,1,0:T(8,128)S(1)} %bitcast.47, ...), custom_call_target="tpu_custom_call" | custom-call | flops 1000 | bytes 1000 | tf_op jit(solution)/shard_map/product/pallas_call | solution.py:167
  74.3 3.2 %collective-permute-start.16 = (f32[256,1536]{1,0:T(8,128)S(1)}, f32[256,1536]{1,0:T(8,128)S(1)}, u32[]{:S(2)}, u32[]{:S(2)}) collective-permute-start(f32[256,1536]{1,0:T(8,128)S(1)} %get-tuple-element.31), channel_id=1, source_target_pairs={{0,192},{1,49},{2,194},{3,51},{4,196},{5,53},{6,198},{7,55},{8,200... | collective-permute-start | bytes 4718600 | tf_op jit(solution)/shard_map/ppermute | solution.py:87
  77.6 7.6 %product.6 = (f32[128,1408]{1,0:T(8,128)S(1)}, f32[128,1408]{1,0:T(8,128)S(1)}, f32[256,1408]{1,0:T(8,128)S(1)}) custom-call(s32[8]{0:T(128)S(1)} %get-tuple-element.48.idx_ref, s32[12]{0:T(128)S(1)} %copy-done, f32[2,32,832]{2,1,0:T(8,128)S(1)} %bitcast.40, f32[2,32,832]{2,1,0:T(8,128)S(1)} %bitcast.48, f32[2,32,832]{2,1,0:T(8,128)S(1)} %bitcast.44, ...), custom_call_target="tpu_custom_call" | custom-call | flops 1000 | bytes 1000 | tf_op jit(solution)/shard_map/product/pallas_call | solution.py:167
  85.2 7.4 %product.7 = (f32[128,1536]{1,0:T(8,128)S(1)}, f32[128,1536]{1,0:T(8,128)S(1)}, f32[256,1536]{1,0:T(8,128)S(1)}) custom-call(s32[8]{0:T(128)S(1)} %get-tuple-element.48.idx_ref, s32[12]{0:T(128)S(1)} %copy-done, f32[2,32,832]{2,1,0:T(8,128)S(1)} %bitcast.41, f32[2,32,832]{2,1,0:T(8,128)S(1)} %bitcast.49, f32[2,32,832]{2,1,0:T(8,128)S(1)} %bitcast.45, ...), custom_call_target="tpu_custom_call" | custom-call | flops 1000 | bytes 1000 | tf_op jit(solution)/shard_map/product/pallas_call | solution.py:167
  92.7 0.1 slice_add_fusion.4
  92.9 3.3 %collective-permute-start.22 = (f32[128,1408]{1,0:T(8,128)S(1)}, f32[128,1408]{1,0:T(8,128)S(1)}, u32[]{:S(2)}, u32[]{:S(2)}) collective-permute-start(f32[128,1408]{1,0:T(8,128)S(1)} %slice_add_fusion.4), channel_id=1, source_target_pairs={{0,192},{1,49},{2,194},{3,51},{4,196},{5,53},{6,198},{7,55},{8,200... | collective-permute-start | bytes 2162696 | tf_op jit(solution)/shard_map/ppermute | solution.py:87
  96.1 2.6 %collective-permute-done.14 = f32[256,1536]{1,0:T(8,128)S(1)} collective-permute-done((f32[256,1536]{1,0:T(8,128)S(1)}, f32[256,1536]{1,0:T(8,128)S(1)}, u32[]{:S(2)}, u32[]{:S(2)}) %collective-permute-start.14) | collective-permute-done | bytes 1572896 | tf_op jit(solution)/shard_map/ppermute | solution.py:87
  98.8 0.1 slice_add_fusion.3
  99.0 0.1 slice_add_fusion
  99.1 3.3 %collective-permute-start.21 = (f32[128,1536]{1,0:T(8,128)S(1)}, f32[128,1536]{1,0:T(8,128)S(1)}, u32[]{:S(2)}, u32[]{:S(2)}) collective-permute-start(f32[128,1536]{1,0:T(8,128)S(1)} %slice_add_fusion), channel_id=1, source_target_pairs={{0,192},{1,49},{2,194},{3,51},{4,196},{5,53},{6,198},{7,55},{8,200... | collective-permute-start | bytes 2359304 | tf_op jit(solution)/shard_map/ppermute | solution.py:87
  102.4 4.1 %collective-permute-done.18 = f32[128,1408]{1,0:T(8,128)S(1)} collective-permute-done((f32[128,1408]{1,0:T(8,128)S(1)}, f32[128,1408]{1,0:T(8,128)S(1)}, u32[]{:S(2)}, u32[]{:S(2)}) %collective-permute-start.18) | collective-permute-done | bytes 720928 | tf_op jit(solution)/shard_map/ppermute | solution.py:87
  106.5 0.2 slice_add_fusion.6
  106.7 8.2 %collective-permute-done.15 = f32[128,1536]{1,0:T(8,128)S(1)} collective-permute-done((f32[128,1536]{1,0:T(8,128)S(1)}, f32[128,1536]{1,0:T(8,128)S(1)}, u32[]{:S(2)}, u32[]{:S(2)}) %collective-permute-start.15) | collective-permute-done | bytes 786464 | tf_op jit(solution)/shard_map/ppermute | solution.py:87
  114.9 0.4 slice_add_fusion.2
  115.4 4.0 %collective-permute-start.20 = (f32[64,2944]{1,0:T(8,128)S(1)}, f32[64,2944]{1,0:T(8,128)S(1)}, u32[]{:S(2)}, u32[]{:S(2)}) collective-permute-start(f32[64,2944]{1,0:T(8,128)S(1)} %pad_maximum_fusion.1), channel_id=1, source_target_pairs={{0,16},{1,65},{2,18},{3,67},{4,20},{5,69},{6,22},{7,71},{8,24},{9,... | collective-permute-start | bytes 2261000 | tf_op jit(solution)/shard_map/ppermute | solution.py:87
  119.4 0.1 fusion.1
  119.5 0.9 collective-permute-start.23
  120.4 1.9 %collective-permute-start.24 = (f32[64,2944]{1,0:T(8,128)S(1)}, f32[64,2944]{1,0:T(8,128)S(1)}, u32[]{:S(2)}, u32[]{:S(2)}) collective-permute-start(f32[64,2944]{1,0:T(8,128)S(1)} %get-tuple-element.40), channel_id=1, source_target_pairs={{0,48},{1,193},{2,50},{3,195},{4,52},{5,197},{6,54},{7,199},{8,56}... | collective-permute-start | bytes 2261000 | tf_op jit(solution)/shard_map/ppermute | solution.py:87
  122.4 14.2 %collective-permute-done.20 = f32[64,2944]{1,0:T(8,128)S(1)} collective-permute-done((f32[64,2944]{1,0:T(8,128)S(1)}, f32[64,2944]{1,0:T(8,128)S(1)}, u32[]{:S(2)}, u32[]{:S(2)}) %collective-permute-start.20) | collective-permute-done | bytes 753696 | tf_op jit(solution)/shard_map/ppermute | solution.py:87
  136.6 3.5 %collective-permute-done.24 = f32[64,2944]{1,0:T(8,128)S(1)} collective-permute-done((f32[64,2944]{1,0:T(8,128)S(1)}, f32[64,2944]{1,0:T(8,128)S(1)}, u32[]{:S(2)}, u32[]{:S(2)}) %collective-permute-start.24) | collective-permute-done | bytes 753696 | tf_op jit(solution)/shard_map/ppermute | solution.py:87
  140.2 1.1 fusion.7
  (36 shorter events, 0.6 us)
Async XLA Ops:
  1.0 10.6 %collective-permute-start = (f32[64,832]{1,0:T(8,128)S(1)}, f32[64,832]{1,0:T(8,128)S(1)}, u32[]{:S(2)}, u32[]{:S(2)}) collective-permute-start(f32[64,832]{1,0:T(8,128)S(1)} %pad_maximum_fusion.5), channel_id=1, source_target_pairs={{0,3},{1,29},{2,47},{3,53},{4,79},{5,89},{6,103},{7,115},{8,135},{... | collective-permute-start | bytes 638984 | tf_op jit(solution)/shard_map/ppermute | solution.py:87
  11.6 4.6 %collective-permute-start.1 = (f32[64,832]{1,0:T(8,128)S(1)}, f32[64,832]{1,0:T(8,128)S(1)}, u32[]{:S(2)}, u32[]{:S(2)}) collective-permute-start(f32[64,832]{1,0:T(8,128)S(1)} %collective-permute-done), channel_id=1, source_target_pairs={{0,1},{1,0},{2,3},{3,2},{4,5},{5,4},{6,7},{7,6},{8,9},{9,8},{10,11... | collective-permute-start | bytes 638984 | tf_op jit(solution)/shard_map/ppermute | solution.py:87
  16.2 9.3 %collective-permute-start.2 = (f32[64,832]{1,0:T(8,128)S(1)}, f32[64,832]{1,0:T(8,128)S(1)}, u32[]{:S(2)}, u32[]{:S(2)}) collective-permute-start(f32[64,832]{1,0:T(8,128)S(1)} %pad_maximum_fusion.6), channel_id=1, source_target_pairs={{0,2},{1,15},{2,4},{3,1},{4,6},{5,3},{6,8},{7,5},{8,10},{9,7},{10,... | collective-permute-start | bytes 638984 | tf_op jit(solution)/shard_map/ppermute | solution.py:87
  19.2 8.8 %collective-permute-start.3 = (f32[64,832]{1,0:T(8,128)S(1)}, f32[64,832]{1,0:T(8,128)S(1)}, u32[]{:S(2)}, u32[]{:S(2)}) collective-permute-start(f32[64,832]{1,0:T(8,128)S(1)} %pad_maximum_fusion.7), channel_id=1, source_target_pairs={{0,2},{1,15},{2,4},{3,1},{4,6},{5,3},{6,8},{7,5},{8,10},{9,7},{10,... | collective-permute-start | bytes 638984 | tf_op jit(solution)/shard_map/ppermute | solution.py:87
  25.5 9.3 %collective-permute-start.4 = (f32[64,832]{1,0:T(8,128)S(1)}, f32[64,832]{1,0:T(8,128)S(1)}, u32[]{:S(2)}, u32[]{:S(2)}) collective-permute-start(f32[64,832]{1,0:T(8,128)S(1)} %collective-permute-done.2), channel_id=1, source_target_pairs={{0,2},{1,15},{2,4},{3,1},{4,6},{5,3},{6,8},{7,5},{8,10},{9,7},{10,... | collective-permute-start | bytes 638984 | tf_op jit(solution)/shard_map/ppermute | solution.py:87
  28.0 9.3 %collective-permute-start.5 = (f32[64,832]{1,0:T(8,128)S(1)}, f32[64,832]{1,0:T(8,128)S(1)}, u32[]{:S(2)}, u32[]{:S(2)}) collective-permute-start(f32[64,832]{1,0:T(8,128)S(1)} %collective-permute-done.3), channel_id=1, source_target_pairs={{0,2},{1,15},{2,4},{3,1},{4,6},{5,3},{6,8},{7,5},{8,10},{9,7},{10,... | collective-permute-start | bytes 638984 | tf_op jit(solution)/shard_map/ppermute | solution.py:87
  34.8 7.2 %collective-permute-start.6 = (f32[64,832]{1,0:T(8,128)S(1)}, f32[64,832]{1,0:T(8,128)S(1)}, u32[]{:S(2)}, u32[]{:S(2)}) collective-permute-start(f32[64,832]{1,0:T(8,128)S(1)} %collective-permute-done.4), channel_id=1, source_target_pairs={{0,2},{1,15},{2,4},{3,1},{4,6},{5,3},{6,8},{7,5},{8,10},{9,7},{10,... | collective-permute-start | bytes 638984 | tf_op jit(solution)/shard_map/ppermute | solution.py:87
  37.3 7.2 %collective-permute-start.7 = (f32[64,832]{1,0:T(8,128)S(1)}, f32[64,832]{1,0:T(8,128)S(1)}, u32[]{:S(2)}, u32[]{:S(2)}) collective-permute-start(f32[64,832]{1,0:T(8,128)S(1)} %collective-permute-done.5), channel_id=1, source_target_pairs={{0,2},{1,15},{2,4},{3,1},{4,6},{5,3},{6,8},{7,5},{8,10},{9,7},{10,... | collective-permute-start | bytes 638984 | tf_op jit(solution)/shard_map/ppermute | solution.py:87
  37.3 14.9 %copy-start = (s32[12]{0:T(128)S(1)}, s32[12]{0:T(128)}, u32[]{:S(2)}) copy-start(s32[12]{0:T(128)} %live_ref.7) | copy-start | bytes 148
  37.3 13.5 %collective-permute-start.10 = (f32[128,832]{1,0:T(8,128)S(1)}, f32[128,832]{1,0:T(8,128)S(1)}, u32[]{:S(2)}, u32[]{:S(2)}) collective-permute-start(f32[128,832]{1,0:T(8,128)S(1)} %pad_maximum_fusion.2), channel_id=1, source_target_pairs={{0,1},{1,0},{2,3},{3,2},{4,5},{5,4},{6,7},{7,6},{8,9},{9,8},{10,11... | collective-permute-start | bytes 1277960 | tf_op jit(solution)/shard_map/ppermute | solution.py:87
  38.8 12.0 %collective-permute-start.11 = (f32[128,832]{1,0:T(8,128)S(1)}, f32[128,832]{1,0:T(8,128)S(1)}, u32[]{:S(2)}, u32[]{:S(2)}) collective-permute-start(f32[128,832]{1,0:T(8,128)S(1)} %pad_maximum_fusion.3), channel_id=1, source_target_pairs={{0,1},{1,0},{2,3},{3,2},{4,5},{5,4},{6,7},{7,6},{8,9},{9,8},{10,11... | collective-permute-start | bytes 1277960 | tf_op jit(solution)/shard_map/ppermute | solution.py:87
  42.1 6.1 %collective-permute-start.8 = (f32[32,832]{1,0:T(8,128)S(1)}, f32[32,832]{1,0:T(8,128)S(1)}, u32[]{:S(2)}, u32[]{:S(2)}) collective-permute-start(f32[32,832]{1,0:T(8,128)S(1)} %slice.110), channel_id=1, source_target_pairs={{0,2},{1,15},{2,4},{3,1},{4,6},{5,3},{6,8},{7,5},{8,10},{9,7},{10,... | collective-permute-start | bytes 319496 | tf_op jit(solution)/shard_map/ppermute | solution.py:87
  44.5 6.1 %collective-permute-start.9 = (f32[32,832]{1,0:T(8,128)S(1)}, f32[32,832]{1,0:T(8,128)S(1)}, u32[]{:S(2)}, u32[]{:S(2)}) collective-permute-start(f32[32,832]{1,0:T(8,128)S(1)} %slice.111), channel_id=1, source_target_pairs={{0,2},{1,15},{2,4},{3,1},{4,6},{5,3},{6,8},{7,5},{8,10},{9,7},{10,... | collective-permute-start | bytes 319496 | tf_op jit(solution)/shard_map/ppermute | solution.py:87
  44.7 7.5 %collective-permute-start.12 = (f32[128,832]{1,0:T(8,128)S(1)}, f32[128,832]{1,0:T(8,128)S(1)}, u32[]{:S(2)}, u32[]{:S(2)}) collective-permute-start(f32[128,832]{1,0:T(8,128)S(1)} %pad_maximum_fusion.4), channel_id=1, source_target_pairs={{0,1},{1,0},{2,3},{3,2},{4,5},{5,4},{6,7},{7,6},{8,9},{9,8},{10,11... | collective-permute-start | bytes 1277960 | tf_op jit(solution)/shard_map/ppermute | solution.py:87
  50.6 1.6 %collective-permute-start.13 = (f32[64,832]{1,0:T(8,128)S(1)}, f32[64,832]{1,0:T(8,128)S(1)}, u32[]{:S(2)}, u32[]{:S(2)}) collective-permute-start(f32[64,832]{1,0:T(8,128)S(1)} %pad_maximum_fusion.8), channel_id=1, source_target_pairs={{0,1},{1,0},{2,3},{3,2},{4,5},{5,4},{6,7},{7,6},{8,9},{9,8},{10,11... | collective-permute-start | bytes 638984 | tf_op jit(solution)/shard_map/ppermute | solution.py:87
  61.7 30.9 %collective-permute-start.17 = (f32[256,1408]{1,0:T(8,128)S(1)}, f32[256,1408]{1,0:T(8,128)S(1)}, u32[]{:S(2)}, u32[]{:S(2)}) collective-permute-start(f32[256,1408]{1,0:T(8,128)S(1)} %get-tuple-element.34), channel_id=1, source_target_pairs={{0,64},{1,17},{2,66},{3,19},{4,68},{5,21},{6,70},{7,23},{8,72},{9,... | collective-permute-start | bytes 4325384 | tf_op jit(solution)/shard_map/ppermute | solution.py:87
  62.8 30.0 %collective-permute-start.19 = (f32[256,1408]{1,0:T(8,128)S(1)}, f32[256,1408]{1,0:T(8,128)S(1)}, u32[]{:S(2)}, u32[]{:S(2)}) collective-permute-start(f32[256,1408]{1,0:T(8,128)S(1)} %get-tuple-element.35), channel_id=1, source_target_pairs={{0,192},{1,49},{2,194},{3,51},{4,196},{5,53},{6,198},{7,55},{8,200... | collective-permute-start | bytes 4325384 | tf_op jit(solution)/shard_map/ppermute | solution.py:87
  74.3 24.4 %collective-permute-start.14 = (f32[256,1536]{1,0:T(8,128)S(1)}, f32[256,1536]{1,0:T(8,128)S(1)}, u32[]{:S(2)}, u32[]{:S(2)}) collective-permute-start(f32[256,1536]{1,0:T(8,128)S(1)} %get-tuple-element.30), channel_id=1, source_target_pairs={{0,64},{1,17},{2,66},{3,19},{4,68},{5,21},{6,70},{7,23},{8,72},{9,... | collective-permute-start | bytes 4718600 | tf_op jit(solution)/shard_map/ppermute | solution.py:87
  74.3 24.6 %collective-permute-start.16 = (f32[256,1536]{1,0:T(8,128)S(1)}, f32[256,1536]{1,0:T(8,128)S(1)}, u32[]{:S(2)}, u32[]{:S(2)}) collective-permute-start(f32[256,1536]{1,0:T(8,128)S(1)} %get-tuple-element.31), channel_id=1, source_target_pairs={{0,192},{1,49},{2,194},{3,51},{4,196},{5,53},{6,198},{7,55},{8,200... | collective-permute-start | bytes 4718600 | tf_op jit(solution)/shard_map/ppermute | solution.py:87
  92.6 13.8 %collective-permute-start.18 = (f32[128,1408]{1,0:T(8,128)S(1)}, f32[128,1408]{1,0:T(8,128)S(1)}, u32[]{:S(2)}, u32[]{:S(2)}) collective-permute-start(f32[128,1408]{1,0:T(8,128)S(1)} %slice_add_fusion.7), channel_id=1, source_target_pairs={{0,64},{1,17},{2,66},{3,19},{4,68},{5,21},{6,70},{7,23},{8,72},{9,... | collective-permute-start | bytes 2162696 | tf_op jit(solution)/shard_map/ppermute | solution.py:87
  92.9 13.6 %collective-permute-start.22 = (f32[128,1408]{1,0:T(8,128)S(1)}, f32[128,1408]{1,0:T(8,128)S(1)}, u32[]{:S(2)}, u32[]{:S(2)}) collective-permute-start(f32[128,1408]{1,0:T(8,128)S(1)} %slice_add_fusion.4), channel_id=1, source_target_pairs={{0,192},{1,49},{2,194},{3,51},{4,196},{5,53},{6,198},{7,55},{8,200... | collective-permute-start | bytes 2162696 | tf_op jit(solution)/shard_map/ppermute | solution.py:87
  98.9 16.0 %collective-permute-start.15 = (f32[128,1536]{1,0:T(8,128)S(1)}, f32[128,1536]{1,0:T(8,128)S(1)}, u32[]{:S(2)}, u32[]{:S(2)}) collective-permute-start(f32[128,1536]{1,0:T(8,128)S(1)} %slice_add_fusion.3), channel_id=1, source_target_pairs={{0,64},{1,17},{2,66},{3,19},{4,68},{5,21},{6,70},{7,23},{8,72},{9,... | collective-permute-start | bytes 2359304 | tf_op jit(solution)/shard_map/ppermute | solution.py:87
  99.1 15.8 %collective-permute-start.21 = (f32[128,1536]{1,0:T(8,128)S(1)}, f32[128,1536]{1,0:T(8,128)S(1)}, u32[]{:S(2)}, u32[]{:S(2)}) collective-permute-start(f32[128,1536]{1,0:T(8,128)S(1)} %slice_add_fusion), channel_id=1, source_target_pairs={{0,192},{1,49},{2,194},{3,51},{4,196},{5,53},{6,198},{7,55},{8,200... | collective-permute-start | bytes 2359304 | tf_op jit(solution)/shard_map/ppermute | solution.py:87
  115.4 24.8 %copy-start.1 = (f32[64,2944]{1,0:T(8,128)S(1)}, f32[64,2944]{1,0:T(8,128)}, u32[]{:S(2)}) copy-start(f32[64,2944]{1,0:T(8,128)} %param.14) | copy-start | bytes 2260996
  115.4 24.8 %copy-start.2 = (f32[2944]{0:T(1024)S(1)}, f32[2944]{0:T(1024)}, u32[]{:S(2)}) copy-start(f32[2944]{0:T(1024)} %param.16) | copy-start | bytes 35332
  115.4 24.7 %copy-start.3 = (f32[64]{0:T(128)S(1)}, f32[64]{0:T(128)}, u32[]{:S(2)}) copy-start(f32[64]{0:T(128)} %param.15) | copy-start | bytes 772
  115.4 21.2 %collective-permute-start.20 = (f32[64,2944]{1,0:T(8,128)S(1)}, f32[64,2944]{1,0:T(8,128)S(1)}, u32[]{:S(2)}, u32[]{:S(2)}) collective-permute-start(f32[64,2944]{1,0:T(8,128)S(1)} %pad_maximum_fusion.1), channel_id=1, source_target_pairs={{0,16},{1,65},{2,18},{3,67},{4,20},{5,69},{6,22},{7,71},{8,24},{9,... | collective-permute-start | bytes 2261000 | tf_op jit(solution)/shard_map/ppermute | solution.py:87
  119.5 17.1 %collective-permute-start.23 = (f32[64,2944]{1,0:T(8,128)S(1)}, f32[64,2944]{1,0:T(8,128)S(1)}, u32[]{:S(2)}, u32[]{:S(2)}) collective-permute-start(f32[64,2944]{1,0:T(8,128)S(1)} %get-tuple-element.39), channel_id=1, source_target_pairs={{0,32},{1,129},{2,34},{3,131},{4,36},{5,133},{6,38},{7,135},{8,40}... | collective-permute-start | bytes 2261000 | tf_op jit(solution)/shard_map/ppermute | solution.py:87
  120.4 19.7 %collective-permute-start.24 = (f32[64,2944]{1,0:T(8,128)S(1)}, f32[64,2944]{1,0:T(8,128)S(1)}, u32[]{:S(2)}, u32[]{:S(2)}) collective-permute-start(f32[64,2944]{1,0:T(8,128)S(1)} %get-tuple-element.40), channel_id=1, source_target_pairs={{0,48},{1,193},{2,50},{3,195},{4,52},{5,197},{6,54},{7,199},{8,56}... | collective-permute-start | bytes 2261000 | tf_op jit(solution)/shard_map/ppermute | solution.py:87

commit v5 on v4

--- a/solution.py
+++ b/solution.py
@@ -14,7 +14,7 @@
 TILE = 512
 COST = 1000
 STREAMS = 2
-ROUNDS = ((0, 3), (3, 6))
+ROUNDS = ((0, 2), (2, 4), (4, 6))
 ORDER = (
     (2, 0), (2, 1), (1, 2), (1, 3),
     (2, 2), (2, 3), (3, 0), (3, 1),

time: 141 us -> 156 us (1.11)
  Pallas kernels: 33.8 us -> 39.7 us
  starting transfers between devices: 36.9 us -> 42.1 us
  waiting for transfers between devices: 66.2 us -> 68.4 us
    pallas_call x4 -> x6, Pallas kernels: 33.8 us -> 39.7 us  [product(): pl.pallas_call(functools.partial(product_kernel, len(xs), len(deps), cd,...]
    ppermute x25 -> x29, starting transfers between devices: 36.9 us -> 42.1 us  [send(): return lax.ppermute(x, AXES, p)]
    ppermute x25 -> x29, waiting for transfers between devices: 66.2 us -> 68.4 us  [send(): return lax.ppermute(x, AXES, p)]
  transfers between devices with their start and end apart: 25 -> 29, of which waited for: 16 -> 17; matrix products, arithmetic and copies ran while one was open for 1% -> 1% of each run, Pallas kernels for 17% -> 21%
where the time goes in v5:
time: 156 us; the launch traced here: 155 us
  waiting for transfers between devices  68.4 us (44%)
  starting transfers between devices  42.1 us (27%)
  Pallas kernels  39.7 us (25%)
  other arithmetic  3.58 us (2%)
    ppermute x29, waiting for transfers between devices, send(): return lax.ppermute(x, AXES, p)  68.4 us
    ppermute x29, starting transfers between devices, send(): return lax.ppermute(x, AXES, p)  42.1 us
    pallas_call x6, Pallas kernels, product(): pl.pallas_call(functools.partial(product_kernel, len(xs), len(deps), cd,...  39.7 us
  transfers between devices with their start and end apart: 29, of which 17 were waited for; matrix products, arithmetic and copies ran while one was open for 1% of the time, Pallas kernels for 21%

profile of v5, /device:TPU:8, one launch (start us, length us, event | category | flops | bytes accessed | tf_op | source)
XLA Modules:
  0.0 155.2 jit_solution(8418986047493813310)
XLA Ops:
  0.0 1.0 pad_maximum_fusion.5
  1.0 7.1 %collective-permute-start = (f32[64,832]{1,0:T(8,128)S(1)}, f32[64,832]{1,0:T(8,128)S(1)}, u32[]{:S(2)}, u32[]{:S(2)}) collective-permute-start(f32[64,832]{1,0:T(8,128)S(1)} %pad_maximum_fusion.5), channel_id=1, source_target_pairs={{0,3},{1,29},{2,47},{3,53},{4,79},{5,89},{6,103},{7,115},{8,135},{... | collective-permute-start | bytes 638984 | tf_op jit(solution)/shard_map/ppermute | solution.py:87
  8.1 3.5 %collective-permute-done = f32[64,832]{1,0:T(8,128)S(1)} collective-permute-done((f32[64,832]{1,0:T(8,128)S(1)}, f32[64,832]{1,0:T(8,128)S(1)}, u32[]{:S(2)}, u32[]{:S(2)}) %collective-permute-start) | collective-permute-done | bytes 213024 | tf_op jit(solution)/shard_map/ppermute | solution.py:87
  11.6 3.4 %collective-permute-start.1 = (f32[64,832]{1,0:T(8,128)S(1)}, f32[64,832]{1,0:T(8,128)S(1)}, u32[]{:S(2)}, u32[]{:S(2)}) collective-permute-start(f32[64,832]{1,0:T(8,128)S(1)} %collective-permute-done), channel_id=1, source_target_pairs={{0,1},{1,0},{2,3},{3,2},{4,5},{5,4},{6,7},{7,6},{8,9},{9,8},{10,11... | collective-permute-start | bytes 638984 | tf_op jit(solution)/shard_map/ppermute | solution.py:87
  15.0 1.1 collective-permute-done.1
  16.2 3.0 %collective-permute-start.2 = (f32[64,832]{1,0:T(8,128)S(1)}, f32[64,832]{1,0:T(8,128)S(1)}, u32[]{:S(2)}, u32[]{:S(2)}) collective-permute-start(f32[64,832]{1,0:T(8,128)S(1)} %pad_maximum_fusion.6), channel_id=1, source_target_pairs={{0,2},{1,15},{2,4},{3,1},{4,6},{5,3},{6,8},{7,5},{8,10},{9,7},{10,... | collective-permute-start | bytes 638984 | tf_op jit(solution)/shard_map/ppermute | solution.py:87
  19.3 6.2 %collective-permute-done.2 = f32[64,832]{1,0:T(8,128)S(1)} collective-permute-done((f32[64,832]{1,0:T(8,128)S(1)}, f32[64,832]{1,0:T(8,128)S(1)}, u32[]{:S(2)}, u32[]{:S(2)}) %collective-permute-start.2) | collective-permute-done | bytes 213024 | tf_op jit(solution)/shard_map/ppermute | solution.py:87
  25.5 2.5 %collective-permute-done.3 = f32[64,832]{1,0:T(8,128)S(1)} collective-permute-done((f32[64,832]{1,0:T(8,128)S(1)}, f32[64,832]{1,0:T(8,128)S(1)}, u32[]{:S(2)}, u32[]{:S(2)}) %collective-permute-start.3) | collective-permute-done | bytes 213024 | tf_op jit(solution)/shard_map/ppermute | solution.py:87
  28.0 1.0 collective-permute-start.5
  29.0 5.8 %collective-permute-done.4 = f32[64,832]{1,0:T(8,128)S(1)} collective-permute-done((f32[64,832]{1,0:T(8,128)S(1)}, f32[64,832]{1,0:T(8,128)S(1)}, u32[]{:S(2)}, u32[]{:S(2)}) %collective-permute-start.4) | collective-permute-done | bytes 213024 | tf_op jit(solution)/shard_map/ppermute | solution.py:87
  34.8 2.5 %collective-permute-done.5 = f32[64,832]{1,0:T(8,128)S(1)} collective-permute-done((f32[64,832]{1,0:T(8,128)S(1)}, f32[64,832]{1,0:T(8,128)S(1)}, u32[]{:S(2)}, u32[]{:S(2)}) %collective-permute-start.5) | collective-permute-done | bytes 213024 | tf_op jit(solution)/shard_map/ppermute | solution.py:87
  37.3 1.5 collective-permute-start.10
  38.8 0.1 collective-permute-start.11
  38.9 3.1 %collective-permute-done.6 = f32[64,832]{1,0:T(8,128)S(1)} collective-permute-done((f32[64,832]{1,0:T(8,128)S(1)}, f32[64,832]{1,0:T(8,128)S(1)}, u32[]{:S(2)}, u32[]{:S(2)}) %collective-permute-start.6) | collective-permute-done | bytes 213024 | tf_op jit(solution)/shard_map/ppermute | solution.py:87
  42.2 2.4 %collective-permute-done.7 = f32[64,832]{1,0:T(8,128)S(1)} collective-permute-done((f32[64,832]{1,0:T(8,128)S(1)}, f32[64,832]{1,0:T(8,128)S(1)}, u32[]{:S(2)}, u32[]{:S(2)}) %collective-permute-start.7) | collective-permute-done | bytes 213024 | tf_op jit(solution)/shard_map/ppermute | solution.py:87
  44.7 0.3 collective-permute-start.12
  45.0 0.7 constant_dynamic-slice_fusion
  45.7 2.5 %collective-permute-done.8 = f32[32,832]{1,0:T(8,128)S(1)} collective-permute-done((f32[32,832]{1,0:T(8,128)S(1)}, f32[32,832]{1,0:T(8,128)S(1)}, u32[]{:S(2)}, u32[]{:S(2)}) %collective-permute-start.8) | collective-permute-done | bytes 106528 | tf_op jit(solution)/shard_map/ppermute | solution.py:87
  48.2 2.5 %collective-permute-done.9 = f32[32,832]{1,0:T(8,128)S(1)} collective-permute-done((f32[32,832]{1,0:T(8,128)S(1)}, f32[32,832]{1,0:T(8,128)S(1)}, u32[]{:S(2)}, u32[]{:S(2)}) %collective-permute-start.9) | collective-permute-done | bytes 106528 | tf_op jit(solution)/shard_map/ppermute | solution.py:87
  50.8 1.4 collective-permute-done.13
  52.2 7.4 %product.8 = (f32[256,896]{1,0:T(8,128)S(1)}, f32[256,896]{1,0:T(8,128)S(1)}, bf16[768,896]{1,0:T(8,128)(2,1)}, bf16[768,896]{1,0:T(8,128)(2,1)}, bf16[192,896]{1,0:T(8,128)(2,1)}) custom-call(s32[8]{0:T(128)S(1)} %get-tuple-element.65.idx_ref, s32[12]{0:T(128)S(1)} %copy-done, f32[2,32,832]{2,1,0:T(8,128)S(1)} %bitcast.48, f32[2,32,832]{2,1,0:T(8,128)S(1)} %bitcast.60, ...), custom_call_target="tpu_custom_call" | custom-call | flops 1000 | bytes 1000 | tf_op jit(solution)/shard_map/product/pallas_call | solution.py:167
  59.6 1.1 collective-permute-start.20
  60.7 2.2 %collective-permute-start.22 = (f32[256,896]{1,0:T(8,128)S(1)}, f32[256,896]{1,0:T(8,128)S(1)}, u32[]{:S(2)}, u32[]{:S(2)}) collective-permute-start(f32[256,896]{1,0:T(8,128)S(1)} %get-tuple-element.51), channel_id=1, source_target_pairs={{0,192},{1,49},{2,194},{3,51},{4,196},{5,53},{6,198},{7,55},{8,200... | collective-permute-start | bytes 2752520 | tf_op jit(solution)/shard_map/ppermute | solution.py:87
  62.9 7.4 %product.7 = (f32[256,1024]{1,0:T(8,128)S(1)}, f32[256,1024]{1,0:T(8,128)S(1)}, bf16[768,1024]{1,0:T(8,128)(2,1)}, bf16[768,1024]{1,0:T(8,128)(2,1)}, bf16[192,1024]{1,0:T(8,128)(2,1)}) custom-call(s32[8]{0:T(128)S(1)} %get-tuple-element.65.idx_ref, s32[12]{0:T(128)S(1)} %copy-done, f32[2,32,832]{2,1,0:T(8,128)S(1)} %bitcast.49, f32[2,32,832]{2,1,0:T(8,128)S(1)} %bitcast.61, ...), custom_call_target="tpu_custom_call" | custom-call | flops 1000 | bytes 1000 | tf_op jit(solution)/shard_map/product/pallas_call | solution.py:167
  70.3 3.2 %collective-permute-start.19 = (f32[256,1024]{1,0:T(8,128)S(1)}, f32[256,1024]{1,0:T(8,128)S(1)}, u32[]{:S(2)}, u32[]{:S(2)}) collective-permute-start(f32[256,1024]{1,0:T(8,128)S(1)} %get-tuple-element.47), channel_id=1, source_target_pairs={{0,192},{1,49},{2,194},{3,51},{4,196},{5,53},{6,198},{7,55},{8,200... | collective-permute-start | bytes 3145736 | tf_op jit(solution)/shard_map/ppermute | solution.py:87
  73.5 7.5 %product.6 = (f32[256,1024]{1,0:T(8,128)S(1)}, f32[256,1024]{1,0:T(8,128)S(1)}, bf16[768,1024]{1,0:T(8,128)(2,1)}, bf16[768,1024]{1,0:T(8,128)(2,1)}, bf16[192,1024]{1,0:T(8,128)(2,1)}) custom-call(s32[8]{0:T(128)S(1)} %get-tuple-element.65.idx_ref, s32[12]{0:T(128)S(1)} %copy-done, f32[2,32,832]{2,1,0:T(8,128)S(1)} %bitcast.50, f32[2,32,832]{2,1,0:T(8,128)S(1)} %bitcast.62, ...), custom_call_target="tpu_custom_call" | custom-call | flops 1000 | bytes 1000 | tf_op jit(solution)/shard_map/product/pallas_call | solution.py:167
  81.0 5.9 %product.9 = (f32[128,896]{1,0:T(8,128)S(1)}, f32[128,896]{1,0:T(8,128)S(1)}, f32[256,896]{1,0:T(8,128)S(1)}) custom-call(s32[8]{0:T(128)S(1)} %get-tuple-element.66.idx_ref, s32[12]{0:T(128)S(1)} %copy-done, f32[2,32,832]{2,1,0:T(8,128)S(1)} %bitcast.51, f32[2,32,832]{2,1,0:T(8,128)S(1)} %bitcast.63, f32[2,32,832]{2,1,0:T(8,128)S(1)} %bitcast.57, ...), custom_call_target="tpu_custom_call" | custom-call | flops 1000 | bytes 1000 | tf_op jit(solution)/shard_map/product/pallas_call | solution.py:167
  86.9 5.7 %product.10 = (f32[128,1024]{1,0:T(8,128)S(1)}, f32[128,1024]{1,0:T(8,128)S(1)}, f32[256,1024]{1,0:T(8,128)S(1)}) custom-call(s32[8]{0:T(128)S(1)} %get-tuple-element.66.idx_ref, s32[12]{0:T(128)S(1)} %copy-done, f32[2,32,832]{2,1,0:T(8,128)S(1)} %bitcast.52, f32[2,32,832]{2,1,0:T(8,128)S(1)} %bitcast.64, f32[2,32,832]{2,1,0:T(8,128)S(1)} %bitcast.58, ...), custom_call_target="tpu_custom_call" | custom-call | flops 1000 | bytes 1000 | tf_op jit(solution)/shard_map/product/pallas_call | solution.py:167
  92.7 5.7 %product.11 = (f32[128,1024]{1,0:T(8,128)S(1)}, f32[128,1024]{1,0:T(8,128)S(1)}, f32[256,1024]{1,0:T(8,128)S(1)}) custom-call(s32[8]{0:T(128)S(1)} %get-tuple-element.66.idx_ref, s32[12]{0:T(128)S(1)} %copy-done, f32[2,32,832]{2,1,0:T(8,128)S(1)} %bitcast.53, f32[2,32,832]{2,1,0:T(8,128)S(1)} %bitcast.65, f32[2,32,832]{2,1,0:T(8,128)S(1)} %bitcast.59, ...), custom_call_target="tpu_custom_call" | custom-call | flops 1000 | bytes 1000 | tf_op jit(solution)/shard_map/product/pallas_call | solution.py:167
  98.4 3.3 %collective-permute-start.16 = (f32[256,1024]{1,0:T(8,128)S(1)}, f32[256,1024]{1,0:T(8,128)S(1)}, u32[]{:S(2)}, u32[]{:S(2)}) collective-permute-start(f32[256,1024]{1,0:T(8,128)S(1)} %get-tuple-element.43), channel_id=1, source_target_pairs={{0,192},{1,49},{2,194},{3,51},{4,196},{5,53},{6,198},{7,55},{8,200... | collective-permute-start | bytes 3145736 | tf_op jit(solution)/shard_map/ppermute | solution.py:87
  102.0 3.5 %collective-permute-start.26 = (f32[128,896]{1,0:T(8,128)S(1)}, f32[128,896]{1,0:T(8,128)S(1)}, u32[]{:S(2)}, u32[]{:S(2)}) collective-permute-start(f32[128,896]{1,0:T(8,128)S(1)} %slice_add_fusion.9), channel_id=1, source_target_pairs={{0,192},{1,49},{2,194},{3,51},{4,196},{5,53},{6,198},{7,55},{8,200... | collective-permute-start | bytes 1376264 | tf_op jit(solution)/shard_map/ppermute | solution.py:87
  105.7 3.3 %collective-permute-start.25 = (f32[128,1024]{1,0:T(8,128)S(1)}, f32[128,1024]{1,0:T(8,128)S(1)}, u32[]{:S(2)}, u32[]{:S(2)}) collective-permute-start(f32[128,1024]{1,0:T(8,128)S(1)} %slice_add_fusion.1), channel_id=1, source_target_pairs={{0,192},{1,49},{2,194},{3,51},{4,196},{5,53},{6,198},{7,55},{8,200... | collective-permute-start | bytes 1572872 | tf_op jit(solution)/shard_map/ppermute | solution.py:87
  109.1 5.0 %collective-permute-done.16 = f32[256,1024]{1,0:T(8,128)S(1)} collective-permute-done((f32[256,1024]{1,0:T(8,128)S(1)}, f32[256,1024]{1,0:T(8,128)S(1)}, u32[]{:S(2)}, u32[]{:S(2)}) %collective-permute-start.16) | collective-permute-done | bytes 1048608 | tf_op jit(solution)/shard_map/ppermute | solution.py:87
  114.2 3.8 %collective-permute-start.24 = (f32[128,1024]{1,0:T(8,128)S(1)}, f32[128,1024]{1,0:T(8,128)S(1)}, u32[]{:S(2)}, u32[]{:S(2)}) collective-permute-start(f32[128,1024]{1,0:T(8,128)S(1)} %slice_add_fusion.3), channel_id=1, source_target_pairs={{0,192},{1,49},{2,194},{3,51},{4,196},{5,53},{6,198},{7,55},{8,200... | collective-permute-start | bytes 1572872 | tf_op jit(solution)/shard_map/ppermute | solution.py:87
  117.9 1.1 collective-permute-done.26
  119.0 0.2 slice_add_fusion.11
  119.2 5.4 %collective-permute-done.25 = f32[128,1024]{1,0:T(8,128)S(1)} collective-permute-done((f32[128,1024]{1,0:T(8,128)S(1)}, f32[128,1024]{1,0:T(8,128)S(1)}, u32[]{:S(2)}, u32[]{:S(2)}) %collective-permute-start.25) | collective-permute-done | bytes 524320 | tf_op jit(solution)/shard_map/ppermute | solution.py:87
  124.6 0.3 slice_add_fusion.5
  124.9 5.3 %collective-permute-done.24 = f32[128,1024]{1,0:T(8,128)S(1)} collective-permute-done((f32[128,1024]{1,0:T(8,128)S(1)}, f32[128,1024]{1,0:T(8,128)S(1)}, u32[]{:S(2)}, u32[]{:S(2)}) %collective-permute-start.24) | collective-permute-done | bytes 524320 | tf_op jit(solution)/shard_map/ppermute | solution.py:87
  130.2 0.3 slice_add_fusion.7
  130.5 0.1 pad_maximum_fusion.1
  130.7 0.1 pad_maximum_fusion
  130.9 2.0 %collective-permute-start.23 = (f32[64,2944]{1,0:T(8,128)S(1)}, f32[64,2944]{1,0:T(8,128)S(1)}, u32[]{:S(2)}, u32[]{:S(2)}) collective-permute-start(f32[64,2944]{1,0:T(8,128)S(1)} %slice.145), channel_id=1, source_target_pairs={{0,16},{1,65},{2,18},{3,67},{4,20},{5,69},{6,22},{7,71},{8,24},{9,... | collective-permute-start | bytes 2261000 | tf_op jit(solution)/shard_map/ppermute | solution.py:87
  132.9 1.4 collective-permute-start.27
  134.3 1.4 collective-permute-start.28
  135.7 14.5 %collective-permute-done.23 = f32[64,2944]{1,0:T(8,128)S(1)} collective-permute-done((f32[64,2944]{1,0:T(8,128)S(1)}, f32[64,2944]{1,0:T(8,128)S(1)}, u32[]{:S(2)}, u32[]{:S(2)}) %collective-permute-start.23) | collective-permute-done | bytes 753696 | tf_op jit(solution)/shard_map/ppermute | solution.py:87
  150.2 3.9 %collective-permute-done.28 = f32[64,2944]{1,0:T(8,128)S(1)} collective-permute-done((f32[64,2944]{1,0:T(8,128)S(1)}, f32[64,2944]{1,0:T(8,128)S(1)}, u32[]{:S(2)}, u32[]{:S(2)}) %collective-permute-start.28) | collective-permute-done | bytes 753696 | tf_op jit(solution)/shard_map/ppermute | solution.py:87
  154.1 1.1 fusion.3
  (51 shorter events, 1.4 us)
Async XLA Ops:
  1.0 10.6 %collective-permute-start = (f32[64,832]{1,0:T(8,128)S(1)}, f32[64,832]{1,0:T(8,128)S(1)}, u32[]{:S(2)}, u32[]{:S(2)}) collective-permute-start(f32[64,832]{1,0:T(8,128)S(1)} %pad_maximum_fusion.5), channel_id=1, source_target_pairs={{0,3},{1,29},{2,47},{3,53},{4,79},{5,89},{6,103},{7,115},{8,135},{... | collective-permute-start | bytes 638984 | tf_op jit(solution)/shard_map/ppermute | solution.py:87
  11.6 4.6 %collective-permute-start.1 = (f32[64,832]{1,0:T(8,128)S(1)}, f32[64,832]{1,0:T(8,128)S(1)}, u32[]{:S(2)}, u32[]{:S(2)}) collective-permute-start(f32[64,832]{1,0:T(8,128)S(1)} %collective-permute-done), channel_id=1, source_target_pairs={{0,1},{1,0},{2,3},{3,2},{4,5},{5,4},{6,7},{7,6},{8,9},{9,8},{10,11... | collective-permute-start | bytes 638984 | tf_op jit(solution)/shard_map/ppermute | solution.py:87
  16.2 9.3 %collective-permute-start.2 = (f32[64,832]{1,0:T(8,128)S(1)}, f32[64,832]{1,0:T(8,128)S(1)}, u32[]{:S(2)}, u32[]{:S(2)}) collective-permute-start(f32[64,832]{1,0:T(8,128)S(1)} %pad_maximum_fusion.6), channel_id=1, source_target_pairs={{0,2},{1,15},{2,4},{3,1},{4,6},{5,3},{6,8},{7,5},{8,10},{9,7},{10,... | collective-permute-start | bytes 638984 | tf_op jit(solution)/shard_map/ppermute | solution.py:87
  19.2 8.8 %collective-permute-start.3 = (f32[64,832]{1,0:T(8,128)S(1)}, f32[64,832]{1,0:T(8,128)S(1)}, u32[]{:S(2)}, u32[]{:S(2)}) collective-permute-start(f32[64,832]{1,0:T(8,128)S(1)} %pad_maximum_fusion.7), channel_id=1, source_target_pairs={{0,2},{1,15},{2,4},{3,1},{4,6},{5,3},{6,8},{7,5},{8,10},{9,7},{10,... | collective-permute-start | bytes 638984 | tf_op jit(solution)/shard_map/ppermute | solution.py:87
  25.5 9.3 %collective-permute-start.4 = (f32[64,832]{1,0:T(8,128)S(1)}, f32[64,832]{1,0:T(8,128)S(1)}, u32[]{:S(2)}, u32[]{:S(2)}) collective-permute-start(f32[64,832]{1,0:T(8,128)S(1)} %collective-permute-done.2), channel_id=1, source_target_pairs={{0,2},{1,15},{2,4},{3,1},{4,6},{5,3},{6,8},{7,5},{8,10},{9,7},{10,... | collective-permute-start | bytes 638984 | tf_op jit(solution)/shard_map/ppermute | solution.py:87
  28.0 9.3 %collective-permute-start.5 = (f32[64,832]{1,0:T(8,128)S(1)}, f32[64,832]{1,0:T(8,128)S(1)}, u32[]{:S(2)}, u32[]{:S(2)}) collective-permute-start(f32[64,832]{1,0:T(8,128)S(1)} %collective-permute-done.3), channel_id=1, source_target_pairs={{0,2},{1,15},{2,4},{3,1},{4,6},{5,3},{6,8},{7,5},{8,10},{9,7},{10,... | collective-permute-start | bytes 638984 | tf_op jit(solution)/shard_map/ppermute | solution.py:87
  34.8 7.2 %collective-permute-start.6 = (f32[64,832]{1,0:T(8,128)S(1)}, f32[64,832]{1,0:T(8,128)S(1)}, u32[]{:S(2)}, u32[]{:S(2)}) collective-permute-start(f32[64,832]{1,0:T(8,128)S(1)} %collective-permute-done.4), channel_id=1, source_target_pairs={{0,2},{1,15},{2,4},{3,1},{4,6},{5,3},{6,8},{7,5},{8,10},{9,7},{10,... | collective-permute-start | bytes 638984 | tf_op jit(solution)/shard_map/ppermute | solution.py:87
  37.3 7.2 %collective-permute-start.7 = (f32[64,832]{1,0:T(8,128)S(1)}, f32[64,832]{1,0:T(8,128)S(1)}, u32[]{:S(2)}, u32[]{:S(2)}) collective-permute-start(f32[64,832]{1,0:T(8,128)S(1)} %collective-permute-done.5), channel_id=1, source_target_pairs={{0,2},{1,15},{2,4},{3,1},{4,6},{5,3},{6,8},{7,5},{8,10},{9,7},{10,... | collective-permute-start | bytes 638984 | tf_op jit(solution)/shard_map/ppermute | solution.py:87
  37.3 14.9 %copy-start = (s32[12]{0:T(128)S(1)}, s32[12]{0:T(128)}, u32[]{:S(2)}) copy-start(s32[12]{0:T(128)} %live_ref.11) | copy-start | bytes 148
  37.3 13.5 %collective-permute-start.10 = (f32[128,832]{1,0:T(8,128)S(1)}, f32[128,832]{1,0:T(8,128)S(1)}, u32[]{:S(2)}, u32[]{:S(2)}) collective-permute-start(f32[128,832]{1,0:T(8,128)S(1)} %pad_maximum_fusion.2), channel_id=1, source_target_pairs={{0,1},{1,0},{2,3},{3,2},{4,5},{5,4},{6,7},{7,6},{8,9},{9,8},{10,11... | collective-permute-start | bytes 1277960 | tf_op jit(solution)/shard_map/ppermute | solution.py:87
  38.8 12.0 %collective-permute-start.11 = (f32[128,832]{1,0:T(8,128)S(1)}, f32[128,832]{1,0:T(8,128)S(1)}, u32[]{:S(2)}, u32[]{:S(2)}) collective-permute-start(f32[128,832]{1,0:T(8,128)S(1)} %pad_maximum_fusion.3), channel_id=1, source_target_pairs={{0,1},{1,0},{2,3},{3,2},{4,5},{5,4},{6,7},{7,6},{8,9},{9,8},{10,11... | collective-permute-start | bytes 1277960 | tf_op jit(solution)/shard_map/ppermute | solution.py:87
  42.1 6.1 %collective-permute-start.8 = (f32[32,832]{1,0:T(8,128)S(1)}, f32[32,832]{1,0:T(8,128)S(1)}, u32[]{:S(2)}, u32[]{:S(2)}) collective-permute-start(f32[32,832]{1,0:T(8,128)S(1)} %slice.136), channel_id=1, source_target_pairs={{0,2},{1,15},{2,4},{3,1},{4,6},{5,3},{6,8},{7,5},{8,10},{9,7},{10,... | collective-permute-start | bytes 319496 | tf_op jit(solution)/shard_map/ppermute | solution.py:87
  44.5 6.1 %collective-permute-start.9 = (f32[32,832]{1,0:T(8,128)S(1)}, f32[32,832]{1,0:T(8,128)S(1)}, u32[]{:S(2)}, u32[]{:S(2)}) collective-permute-start(f32[32,832]{1,0:T(8,128)S(1)} %slice.137), channel_id=1, source_target_pairs={{0,2},{1,15},{2,4},{3,1},{4,6},{5,3},{6,8},{7,5},{8,10},{9,7},{10,... | collective-permute-start | bytes 319496 | tf_op jit(solution)/shard_map/ppermute | solution.py:87
  44.7 7.5 %collective-permute-start.12 = (f32[128,832]{1,0:T(8,128)S(1)}, f32[128,832]{1,0:T(8,128)S(1)}, u32[]{:S(2)}, u32[]{:S(2)}) collective-permute-start(f32[128,832]{1,0:T(8,128)S(1)} %pad_maximum_fusion.4), channel_id=1, source_target_pairs={{0,1},{1,0},{2,3},{3,2},{4,5},{5,4},{6,7},{7,6},{8,9},{9,8},{10,11... | collective-permute-start | bytes 1277960 | tf_op jit(solution)/shard_map/ppermute | solution.py:87
  50.6 1.6 %collective-permute-start.13 = (f32[64,832]{1,0:T(8,128)S(1)}, f32[64,832]{1,0:T(8,128)S(1)}, u32[]{:S(2)}, u32[]{:S(2)}) collective-permute-start(f32[64,832]{1,0:T(8,128)S(1)} %pad_maximum_fusion.8), channel_id=1, source_target_pairs={{0,1},{1,0},{2,3},{3,2},{4,5},{5,4},{6,7},{7,6},{8,9},{9,8},{10,11... | collective-permute-start | bytes 638984 | tf_op jit(solution)/shard_map/ppermute | solution.py:87
  59.6 38.8 %collective-permute-start.20 = (f32[256,896]{1,0:T(8,128)S(1)}, f32[256,896]{1,0:T(8,128)S(1)}, u32[]{:S(2)}, u32[]{:S(2)}) collective-permute-start(f32[256,896]{1,0:T(8,128)S(1)} %get-tuple-element.50), channel_id=1, source_target_pairs={{0,64},{1,17},{2,66},{3,19},{4,68},{5,21},{6,70},{7,23},{8,72},{9,... | collective-permute-start | bytes 2752520 | tf_op jit(solution)/shard_map/ppermute | solution.py:87
  60.7 41.1 %collective-permute-start.22 = (f32[256,896]{1,0:T(8,128)S(1)}, f32[256,896]{1,0:T(8,128)S(1)}, u32[]{:S(2)}, u32[]{:S(2)}) collective-permute-start(f32[256,896]{1,0:T(8,128)S(1)} %get-tuple-element.51), channel_id=1, source_target_pairs={{0,192},{1,49},{2,194},{3,51},{4,196},{5,53},{6,198},{7,55},{8,200... | collective-permute-start | bytes 2752520 | tf_op jit(solution)/shard_map/ppermute | solution.py:87
  70.3 31.7 %collective-permute-start.17 = (f32[256,1024]{1,0:T(8,128)S(1)}, f32[256,1024]{1,0:T(8,128)S(1)}, u32[]{:S(2)}, u32[]{:S(2)}) collective-permute-start(f32[256,1024]{1,0:T(8,128)S(1)} %get-tuple-element.46), channel_id=1, source_target_pairs={{0,64},{1,17},{2,66},{3,19},{4,68},{5,21},{6,70},{7,23},{8,72},{9,... | collective-permute-start | bytes 3145736 | tf_op jit(solution)/shard_map/ppermute | solution.py:87
  70.3 35.2 %collective-permute-start.19 = (f32[256,1024]{1,0:T(8,128)S(1)}, f32[256,1024]{1,0:T(8,128)S(1)}, u32[]{:S(2)}, u32[]{:S(2)}) collective-permute-start(f32[256,1024]{1,0:T(8,128)S(1)} %get-tuple-element.47), channel_id=1, source_target_pairs={{0,192},{1,49},{2,194},{3,51},{4,196},{5,53},{6,198},{7,55},{8,200... | collective-permute-start | bytes 3145736 | tf_op jit(solution)/shard_map/ppermute | solution.py:87
  81.0 24.7 %collective-permute-start.14 = (f32[256,1024]{1,0:T(8,128)S(1)}, f32[256,1024]{1,0:T(8,128)S(1)}, u32[]{:S(2)}, u32[]{:S(2)}) collective-permute-start(f32[256,1024]{1,0:T(8,128)S(1)} %get-tuple-element.42), channel_id=1, source_target_pairs={{0,64},{1,17},{2,66},{3,19},{4,68},{5,21},{6,70},{7,23},{8,72},{9,... | collective-permute-start | bytes 3145736 | tf_op jit(solution)/shard_map/ppermute | solution.py:87
  98.4 15.6 %collective-permute-start.16 = (f32[256,1024]{1,0:T(8,128)S(1)}, f32[256,1024]{1,0:T(8,128)S(1)}, u32[]{:S(2)}, u32[]{:S(2)}) collective-permute-start(f32[256,1024]{1,0:T(8,128)S(1)} %get-tuple-element.43), channel_id=1, source_target_pairs={{0,192},{1,49},{2,194},{3,51},{4,196},{5,53},{6,198},{7,55},{8,200... | collective-permute-start | bytes 3145736 | tf_op jit(solution)/shard_map/ppermute | solution.py:87
  101.8 12.3 %collective-permute-start.21 = (f32[128,896]{1,0:T(8,128)S(1)}, f32[128,896]{1,0:T(8,128)S(1)}, u32[]{:S(2)}, u32[]{:S(2)}) collective-permute-start(f32[128,896]{1,0:T(8,128)S(1)} %slice_add_fusion.12), channel_id=1, source_target_pairs={{0,64},{1,17},{2,66},{3,19},{4,68},{5,21},{6,70},{7,23},{8,72},{9,... | collective-permute-start | bytes 1376264 | tf_op jit(solution)/shard_map/ppermute | solution.py:87
  102.0 17.0 %collective-permute-start.26 = (f32[128,896]{1,0:T(8,128)S(1)}, f32[128,896]{1,0:T(8,128)S(1)}, u32[]{:S(2)}, u32[]{:S(2)}) collective-permute-start(f32[128,896]{1,0:T(8,128)S(1)} %slice_add_fusion.9), channel_id=1, source_target_pairs={{0,192},{1,49},{2,194},{3,51},{4,196},{5,53},{6,198},{7,55},{8,200... | collective-permute-start | bytes 1376264 | tf_op jit(solution)/shard_map/ppermute | solution.py:87
  105.6 13.6 %collective-permute-start.18 = (f32[128,1024]{1,0:T(8,128)S(1)}, f32[128,1024]{1,0:T(8,128)S(1)}, u32[]{:S(2)}, u32[]{:S(2)}) collective-permute-start(f32[128,1024]{1,0:T(8,128)S(1)} %slice_add_fusion.6), channel_id=1, source_target_pairs={{0,64},{1,17},{2,66},{3,19},{4,68},{5,21},{6,70},{7,23},{8,72},{9,... | collective-permute-start | bytes 1572872 | tf_op jit(solution)/shard_map/ppermute | solution.py:87
  105.7 18.8 %collective-permute-start.25 = (f32[128,1024]{1,0:T(8,128)S(1)}, f32[128,1024]{1,0:T(8,128)S(1)}, u32[]{:S(2)}, u32[]{:S(2)}) collective-permute-start(f32[128,1024]{1,0:T(8,128)S(1)} %slice_add_fusion.1), channel_id=1, source_target_pairs={{0,192},{1,49},{2,194},{3,51},{4,196},{5,53},{6,198},{7,55},{8,200... | collective-permute-start | bytes 1572872 | tf_op jit(solution)/shard_map/ppermute | solution.py:87
  114.1 10.9 %collective-permute-start.15 = (f32[128,1024]{1,0:T(8,128)S(1)}, f32[128,1024]{1,0:T(8,128)S(1)}, u32[]{:S(2)}, u32[]{:S(2)}) collective-permute-start(f32[128,1024]{1,0:T(8,128)S(1)} %slice_add_fusion.8), channel_id=1, source_target_pairs={{0,64},{1,17},{2,66},{3,19},{4,68},{5,21},{6,70},{7,23},{8,72},{9,... | collective-permute-start | bytes 1572872 | tf_op jit(solution)/shard_map/ppermute | solution.py:87
  114.2 16.1 %collective-permute-start.24 = (f32[128,1024]{1,0:T(8,128)S(1)}, f32[128,1024]{1,0:T(8,128)S(1)}, u32[]{:S(2)}, u32[]{:S(2)}) collective-permute-start(f32[128,1024]{1,0:T(8,128)S(1)} %slice_add_fusion.3), channel_id=1, source_target_pairs={{0,192},{1,49},{2,194},{3,51},{4,196},{5,53},{6,198},{7,55},{8,200... | collective-permute-start | bytes 1572872 | tf_op jit(solution)/shard_map/ppermute | solution.py:87
  130.8 23.2 %copy-start.1 = (f32[64,2944]{1,0:T(8,128)S(1)}, f32[64,2944]{1,0:T(8,128)}, u32[]{:S(2)}) copy-start(f32[64,2944]{1,0:T(8,128)} %param.14) | copy-start | bytes 2260996
  130.8 23.2 %copy-start.2 = (f32[2944]{0:T(1024)S(1)}, f32[2944]{0:T(1024)}, u32[]{:S(2)}) copy-start(f32[2944]{0:T(1024)} %param.16) | copy-start | bytes 35332
  130.9 23.2 %copy-start.3 = (f32[64]{0:T(128)S(1)}, f32[64]{0:T(128)}, u32[]{:S(2)}) copy-start(f32[64]{0:T(128)} %param.15) | copy-start | bytes 772
  130.9 19.3 %collective-permute-start.23 = (f32[64,2944]{1,0:T(8,128)S(1)}, f32[64,2944]{1,0:T(8,128)S(1)}, u32[]{:S(2)}, u32[]{:S(2)}) collective-permute-start(f32[64,2944]{1,0:T(8,128)S(1)} %slice.145), channel_id=1, source_target_pairs={{0,16},{1,65},{2,18},{3,67},{4,20},{5,69},{6,22},{7,71},{8,24},{9,... | collective-permute-start | bytes 2261000 | tf_op jit(solution)/shard_map/ppermute | solution.py:87
  132.9 17.3 %collective-permute-start.27 = (f32[64,2944]{1,0:T(8,128)S(1)}, f32[64,2944]{1,0:T(8,128)S(1)}, u32[]{:S(2)}, u32[]{:S(2)}) collective-permute-start(f32[64,2944]{1,0:T(8,128)S(1)} %get-tuple-element.53), channel_id=1, source_target_pairs={{0,32},{1,129},{2,34},{3,131},{4,36},{5,133},{6,38},{7,135},{8,40}... | collective-permute-start | bytes 2261000 | tf_op jit(solution)/shard_map/ppermute | solution.py:87
  134.3 19.7 %collective-permute-start.28 = (f32[64,2944]{1,0:T(8,128)S(1)}, f32[64,2944]{1,0:T(8,128)S(1)}, u32[]{:S(2)}, u32[]{:S(2)}) collective-permute-start(f32[64,2944]{1,0:T(8,128)S(1)} %get-tuple-element.54), channel_id=1, source_target_pairs={{0,48},{1,193},{2,50},{3,195},{4,52},{5,197},{6,54},{7,199},{8,56}... | collective-permute-start | bytes 2261000 | tf_op jit(solution)/shard_map/ppermute | solution.py:87
